TPU v7x, 512 devices: a whole 4x4x16 slice. The times are simulated.
512 devices in a mesh: section: 8 (over z_hi, x), dp: 64 (over z_lo, y, core).
Axes of the slice: x: 4, y: 4, z: 16 (z_hi: 2, z_lo: 8; z = z_hi * 8 + z_lo), core: 2. Of those that a mesh axis runs over, the one named last changes fastest.
Arguments:
- inputs: bfloat16 [8192, 512], P('dp'), may hold values from -16 to 16
- targets: bfloat16 [8192, 512], P('dp'), may hold values from -6 to 6
- w_in: bfloat16 [8, 512, 2048], P('section', 'dp'), may hold values from -0.25 to 0.25
- w_out: bfloat16 [8, 2048, 512], P('section', 'dp'), may hold values from -0.125 to 0.125
- probes: bfloat16 [8, 512, 2048], P('section'), may hold values from -1 to 1, as said below
Outputs:
- diagonal: float32 [8, 512, 2048], P('section', 'dp')
Inputs may be any that keep to these rules, and one draw needn't show every extreme that they name: `probes`: every entry is -1 or +1.
All inputs are finite; a program needn't handle non-finite values.
Results may differ from a plain program's by a relative error of at most 0.01.
Values may be sent and summed in bfloat16 or wider, within the bound.
No kernel may reach another device: no remote copies, remote signals or barrier semaphores. Data moves between devices by JAX's collectives and lax.ppermute only.
A program may use at most 64 MiB of HBM per device.

v0:
```python
import jax
import jax.numpy as jnp
from jax import lax
from jax.sharding import PartitionSpec as P

MICRO = 2


EPSILON = 1e-05
SQRT_HALF = 0.7071067811865476
INV_ROOT_TWO_PI = 0.3989422804014327
CONTRACT_LAST = (((1,), (1,)), ((), ()))
CONTRACT_FIRST = (((0,), (0,)), ((), ()))


def passed_along(value, axis, by):
    length = lax.axis_size(axis)
    pairs = [(i, i + by) for i in range(length) if 0 <= i + by < length]
    return lax.ppermute(value, axis, pairs)


def row_mean(values):
    return jnp.mean(values, axis=-1, keepdims=True)


def gelu_terms(preact):
    normal_cdf = 0.5 * (1.0 + lax.erf(preact * SQRT_HALF))
    density = INV_ROOT_TWO_PI * jnp.exp(-0.5 * preact * preact)
    return (preact * normal_cdf, normal_cdf + preact * density, density * (2.0 - preact * preact))


def forward_layer(inflow, inflow_t, weight_in, weight_out, probe_mat):
    centred = inflow - row_mean(inflow)
    rscale = lax.rsqrt(row_mean(centred * centred) + EPSILON)
    normed = centred * rscale
    tangent_dot = row_mean(normed * inflow_t)
    normed_t = rscale * (inflow_t - row_mean(inflow_t) - normed * tangent_dot)
    low_normed = normed.astype(jnp.bfloat16)
    preact = jnp.dot(low_normed, weight_in, preferred_element_type=jnp.float32)
    preact_t = jnp.dot(
        normed_t.astype(jnp.bfloat16), weight_in, preferred_element_type=jnp.float32
    ) + jnp.dot(low_normed, probe_mat, preferred_element_type=jnp.float32)
    activation, slope_one, slope_two = gelu_terms(preact)
    hidden = activation.astype(jnp.bfloat16)
    hidden_t = (slope_one * preact_t).astype(jnp.bfloat16)
    outflow = inflow + jnp.dot(hidden, weight_out, preferred_element_type=jnp.float32)
    outflow_t = inflow_t + jnp.dot(hidden_t, weight_out, preferred_element_type=jnp.float32)
    return (outflow, outflow_t, (normed, normed_t, rscale, tangent_dot, preact, preact_t))


def norm_apply(values, normed, rscale):
    return rscale * (values - row_mean(values) - normed * row_mean(normed * values))


def backward_layer(adjoint, adjoint_t, stored, weight_in, weight_out, probe_mat):
    normed, normed_t, rscale, tangent_dot, preact, preact_t = stored
    activation, slope_one, slope_two = gelu_terms(preact)
    grad_hidden = lax.dot_general(
        adjoint, weight_out, CONTRACT_LAST, preferred_element_type=jnp.float32
    )
    grad_hidden_t = lax.dot_general(
        adjoint_t, weight_out, CONTRACT_LAST, preferred_element_type=jnp.float32
    )
    grad_pre = grad_hidden * slope_one
    grad_pre_t = grad_hidden_t * slope_one + grad_hidden * slope_two * preact_t
    low_grad = grad_pre.astype(jnp.bfloat16)
    low_grad_t = grad_pre_t.astype(jnp.bfloat16)
    grad_norm = lax.dot_general(
        low_grad, weight_in, CONTRACT_LAST, preferred_element_type=jnp.float32
    )
    grad_norm_t = lax.dot_general(
        low_grad_t, weight_in, CONTRACT_LAST, preferred_element_type=jnp.float32
    ) + lax.dot_general(low_grad, probe_mat, CONTRACT_LAST, preferred_element_type=jnp.float32)
    through = norm_apply(grad_norm, normed, rscale)
    through_t = (
        norm_apply(grad_norm_t, normed, rscale)
        - rscale * tangent_dot * through
        - rscale
        * (normed_t * row_mean(normed * grad_norm) + normed * row_mean(normed_t * grad_norm))
    )
    return (
        adjoint.astype(jnp.float32) + through,
        adjoint_t.astype(jnp.float32) + through_t,
        low_grad,
        low_grad_t,
    )


def curvature(normed, normed_t, low_grad, low_grad_t):
    first_term = lax.dot_general(
        normed.astype(jnp.bfloat16), low_grad_t, CONTRACT_FIRST, preferred_element_type=jnp.float32
    )
    second_term = lax.dot_general(
        normed_t.astype(jnp.bfloat16), low_grad, CONTRACT_FIRST, preferred_element_type=jnp.float32
    )
    return first_term + second_term


def shards(inputs, targets, w_in, w_out, probes):
    section_index = lax.axis_index("section")
    section_count = lax.axis_size("section")
    gathered_in, gathered_out = (
        lax.all_gather(w_in, "dp", axis=1, tiled=True),
        lax.all_gather(w_out, "dp", axis=1, tiled=True),
    )
    weight_in = gathered_in[0]
    weight_out = gathered_out[0]
    probe_full = probes[0]
    local_rows, feature_width = inputs.shape
    hidden_width = probe_full.shape[1]
    owned_rows = feature_width // lax.axis_size("dp")
    probe_own = lax.dynamic_slice_in_dim(
        probe_full, lax.axis_index("dp") * owned_rows, owned_rows, 0
    )
    micro_rows = local_rows // MICRO
    token_total = local_rows * lax.axis_size("dp")
    first_inputs = inputs.reshape(MICRO, micro_rows, feature_width)
    goal_rows = targets.reshape(MICRO, micro_rows, feature_width)
    tick_count = MICRO + section_count - 1
    wide_zeros = jnp.zeros((MICRO, micro_rows, feature_width), jnp.float32)
    hidden_zeros = jnp.zeros((MICRO, micro_rows, hidden_width), jnp.float32)
    narrow_zeros = jnp.zeros((MICRO, micro_rows, 1), jnp.float32)
    stored_start = (wide_zeros, wide_zeros, narrow_zeros, narrow_zeros, hidden_zeros, hidden_zeros)
    pair_zeros = jnp.zeros((2, micro_rows, feature_width), jnp.bfloat16)
    top_start = jnp.zeros((MICRO, 2, micro_rows, feature_width), jnp.bfloat16)

    def forward_step(tick_now, received, stored_now, top_now):
        micro_index = tick_now - section_index
        active = (micro_index >= 0) & (micro_index < MICRO)
        micro_slot = jnp.clip(micro_index, 0, MICRO - 1)

        def forward_advance(operands):
            stored_old, top_pairs_old = operands
            fresh = lax.dynamic_index_in_dim(first_inputs, micro_slot, 0, keepdims=False)
            inflow = jnp.where(section_index == 0, fresh, received[0]).astype(jnp.float32)
            inflow_t = jnp.where(section_index == 0, jnp.zeros_like(fresh), received[1]).astype(
                jnp.float32
            )
            outflow, outflow_t, pieces = forward_layer(
                inflow, inflow_t, weight_in, weight_out, probe_full
            )
            stored_new = tuple(
                (
                    lax.dynamic_update_index_in_dim(buffer_old, fresh_piece, micro_slot, 0)
                    for buffer_old, fresh_piece in zip(stored_old, pieces)
                )
            )
            goal_now = lax.dynamic_index_in_dim(goal_rows, micro_slot, 0, keepdims=False).astype(
                jnp.float32
            )
            top_pair = jnp.stack(
                [(outflow - goal_now) / token_total, outflow_t / token_total]
            ).astype(jnp.bfloat16)
            top_pairs_new = lax.dynamic_update_index_in_dim(top_pairs_old, top_pair, micro_slot, 0)
            return (jnp.stack([outflow, outflow_t]).astype(jnp.bfloat16), stored_new, top_pairs_new)

        def forward_unchanged(operands):
            return (pair_zeros, operands[0], operands[1])

        return lax.cond(active, forward_advance, forward_unchanged, (stored_now, top_now))

    def forward_tick(tick_now, state_now):
        received, stored_now, top_now = state_now
        sending, stored_now, top_now = forward_step(tick_now, received, stored_now, top_now)
        received = passed_along(sending, "section", 1)
        return (received, stored_now, top_now)

    received, stored, top_pairs = lax.fori_loop(
        0, tick_count - 1, forward_tick, (pair_zeros, stored_start, top_start)
    )
    leftover, stored, top_pairs = forward_step(tick_count - 1, received, stored, top_pairs)
    curvature_start = jnp.zeros((feature_width, hidden_width), jnp.float32)

    def backward_step(tick_now, received_now, curvature_state):
        micro_index = tick_now - (section_count - 1 - section_index)
        active = (micro_index >= 0) & (micro_index < MICRO)
        micro_slot = jnp.clip(micro_index, 0, MICRO - 1)

        def backward_advance(held_state):
            pieces = tuple(
                (
                    lax.dynamic_index_in_dim(buffer_old, micro_slot, 0, keepdims=False)
                    for buffer_old in stored
                )
            )
            top_pair = lax.dynamic_index_in_dim(top_pairs, micro_slot, 0, keepdims=False)
            incoming = jnp.where(section_index == section_count - 1, top_pair, received_now)
            upstream, upstream_t, low_grad, low_grad_t = backward_layer(
                incoming[0], incoming[1], pieces, weight_in, weight_out, probe_full
            )
            sending_now = jnp.stack([upstream, upstream_t]).astype(jnp.bfloat16)
            held_state = held_state + curvature(pieces[0], pieces[1], low_grad, low_grad_t)
            return (sending_now, held_state)

        def backward_unchanged(held_state):
            return (pair_zeros, held_state)

        return lax.cond(active, backward_advance, backward_unchanged, curvature_state)

    def backward_tick(tick_now, state_now):
        received_now, curvature_state = state_now
        sending, curvature_state = backward_step(tick_now, received_now, curvature_state)
        received_now = passed_along(sending, "section", -1)
        return (received_now, curvature_state)

    received, curvature_state = lax.fori_loop(
        0, tick_count - 1, backward_tick, (pair_zeros, curvature_start)
    )
    leftover, curvature_state = backward_step(tick_count - 1, received, curvature_state)
    hessian_own = lax.psum_scatter(curvature_state, "dp", scatter_dimension=0, tiled=True)
    return (probe_own.astype(jnp.float32) * hessian_own)[None]


def solution(mesh):
    return jax.shard_map(
        shards,
        mesh=mesh,
        in_specs=(
            P("dp", None),
            P("dp", None),
            P("section", "dp", None),
            P("section", "dp", None),
            P("section", None, None),
        ),
        out_specs=P("section", "dp", None),
        check_vma=False,
    )
```

profile of v0, /device:TPU:2, one launch (start us, length us, event | category | flops | bytes accessed | tf_op | source)
XLA Modules:
  0.0 1047.8 jit_solution(9384231018857720913)
XLA Ops:
  8.1 126.6 %all-gather.3.cloned.1.call-done = bf16[1,512,2048]{2,1,0:T(8,128)(2,1)} async-done(((bf16[1,8,2048]{2,1,0:T(8,128)(2,1)}), bf16[1,512,2048]{2,1,0:T(8,128)(2,1)}) %all-gather.3.cloned.1.call-update) | async-done | bytes 2097168 | tf_op jit(solution)/shard_map/all_gather | solution.py:103
  134.7 118.7 %all-gather.5.cloned.1.call-done = bf16[1,2048,512]{2,1,0:T(8,128)(2,1)} async-done(((bf16[1,32,512]{2,1,0:T(8,128)(2,1)}), bf16[1,2048,512]{2,1,0:T(8,128)(2,1)}) %all-gather.5.cloned.1.call-update) | async-done | bytes 2097168 | tf_op jit(solution)/shard_map/all_gather | solution.py:104
  256.2 135.4 %while.49 = (s32[]{:T(128)}, bf16[2,64,512]{2,1,0:T(8,128)(2,1)S(1)}, f32[2,64,512]{2,1,0:T(8,128)}, f32[2,64,512]{2,1,0:T(8,128)S(1)}, f32[2,64,1]{1,2,0:T(1,12...) while((s32[]{:T(128)}, ...), condition=%wide.region_7.8_spmd, body=%wide.region_0.7_spmd.sunk | while | flops 675381504 | bytes 47723040 | solution.py:168
  256.9 3.4 collective-permute-start
  260.3 10.6 %collective-permute-done = bf16[2,64,512]{2,1,0:T(8,128)(2,1)S(1)} collective-permute-done((bf16[2,64,512]{2,1,0:T(8,128)(2,1)}, bf16[2,64,512]{2,1,0:T(8,128)(2,1)S(1)}, u32[]{:S(2)}, u32[]{:S(2)}) %collective-permute-start) | collective-permute-done | bytes 131104 | tf_op jit(solution)/shard_map/while/body/eval_jaxpr/ppermute | solution.py:19
  270.9 8.6 conditional.8
  272.4 2.1 fusion.31
  279.5 1.9 collective-permute-start
  281.4 5.3 collective-permute-done
  286.7 8.6 conditional.8
  288.3 2.1 fusion.31
  295.4 2.2 collective-permute-start
  297.6 4.9 collective-permute-done
  303.1 10.1 collective-permute-start
  313.2 2.8 collective-permute-done
  316.7 8.2 collective-permute-start
  324.9 2.8 collective-permute-done
  328.4 15.1 %collective-permute-start = (bf16[2,64,512]{2,1,0:T(8,128)(2,1)}, bf16[2,64,512]{2,1,0:T(8,128)(2,1)S(1)}, u32[]{:S(2)}, u32[]{:S(2)}) collective-permute-start(bf16[2,64,512]{2,1,0:T(8,128)(2,1)} %get-tuple-element.1100), channel_id=1, source_target_pairs={{0,64},{64,128},{128,192},{192,256},{256,320},{320,384},{384,448},... | collective-permute-start | bytes 393224 | tf_op jit(solution)/shard_map/while/body/eval_jaxpr/ppermute | solution.py:19
  343.5 2.8 collective-permute-done
  347.0 15.2 %collective-permute-start = (bf16[2,64,512]{2,1,0:T(8,128)(2,1)}, bf16[2,64,512]{2,1,0:T(8,128)(2,1)S(1)}, u32[]{:S(2)}, u32[]{:S(2)}) collective-permute-start(bf16[2,64,512]{2,1,0:T(8,128)(2,1)} %get-tuple-element.1100), channel_id=1, source_target_pairs={{0,64},{64,128},{128,192},{192,256},{256,320},{320,384},{384,448},... | collective-permute-start | bytes 393224 | tf_op jit(solution)/shard_map/while/body/eval_jaxpr/ppermute | solution.py:19
  362.1 2.8 collective-permute-done
  365.6 23.1 %collective-permute-start = (bf16[2,64,512]{2,1,0:T(8,128)(2,1)}, bf16[2,64,512]{2,1,0:T(8,128)(2,1)S(1)}, u32[]{:S(2)}, u32[]{:S(2)}) collective-permute-start(bf16[2,64,512]{2,1,0:T(8,128)(2,1)} %get-tuple-element.1100), channel_id=1, source_target_pairs={{0,64},{64,128},{128,192},{192,256},{256,320},{320,384},{384,448},... | collective-permute-start | bytes 393224 | tf_op jit(solution)/shard_map/while/body/eval_jaxpr/ppermute | solution.py:19
  388.8 2.8 collective-permute-done
  391.6 2.5 broadcast_in_dim.68
  394.1 185.6 %while.50 = (s32[]{:T(128)}, bf16[2,64,512]{2,1,0:T(8,128)(2,1)S(1)}, f32[512,2048]{1,0:T(8,128)}, s32[]{:T(128)}, s32[]{:T(128)}, /*index=5*/bf16[2,2,64,512]{3...) while((s32[]{:T(128)}, ...), condition=%wide.region_22.23_spmd, body=%wide.region_14.22_spmd.sunk | while | flops 946143296 | bytes 90446936 | solution.py:206
  394.8 1.9 collective-permute-start.1
  396.7 16.4 %collective-permute-done.1 = bf16[2,64,512]{2,1,0:T(8,128)(2,1)S(1)} collective-permute-done((bf16[2,64,512]{2,1,0:T(8,128)(2,1)}, bf16[2,64,512]{2,1,0:T(8,128)(2,1)S(1)}, u32[]{:S(2)}, u32[]{:S(2)}) %collective-permute-start.1) | collective-permute-done | bytes 131104 | tf_op jit(solution)/shard_map/while/body/eval_jaxpr/ppermute | solution.py:19
  413.8 1.9 collective-permute-start.1
  415.7 16.4 %collective-permute-done.1 = bf16[2,64,512]{2,1,0:T(8,128)(2,1)S(1)} collective-permute-done((bf16[2,64,512]{2,1,0:T(8,128)(2,1)}, bf16[2,64,512]{2,1,0:T(8,128)(2,1)S(1)}, u32[]{:S(2)}, u32[]{:S(2)}) %collective-permute-start.1) | collective-permute-done | bytes 131104 | tf_op jit(solution)/shard_map/while/body/eval_jaxpr/ppermute | solution.py:19
  432.7 1.9 collective-permute-start.1
  434.7 16.5 %collective-permute-done.1 = bf16[2,64,512]{2,1,0:T(8,128)(2,1)S(1)} collective-permute-done((bf16[2,64,512]{2,1,0:T(8,128)(2,1)}, bf16[2,64,512]{2,1,0:T(8,128)(2,1)S(1)}, u32[]{:S(2)}, u32[]{:S(2)}) %collective-permute-start.1) | collective-permute-done | bytes 131104 | tf_op jit(solution)/shard_map/while/body/eval_jaxpr/ppermute | solution.py:19
  451.8 1.9 collective-permute-start.1
  453.7 16.1 %collective-permute-done.1 = bf16[2,64,512]{2,1,0:T(8,128)(2,1)S(1)} collective-permute-done((bf16[2,64,512]{2,1,0:T(8,128)(2,1)}, bf16[2,64,512]{2,1,0:T(8,128)(2,1)S(1)}, u32[]{:S(2)}, u32[]{:S(2)}) %collective-permute-start.1) | collective-permute-done | bytes 131104 | tf_op jit(solution)/shard_map/while/body/eval_jaxpr/ppermute | solution.py:19
  470.5 1.9 collective-permute-start.1
  472.4 16.1 %collective-permute-done.1 = bf16[2,64,512]{2,1,0:T(8,128)(2,1)S(1)} collective-permute-done((bf16[2,64,512]{2,1,0:T(8,128)(2,1)}, bf16[2,64,512]{2,1,0:T(8,128)(2,1)S(1)}, u32[]{:S(2)}, u32[]{:S(2)}) %collective-permute-start.1) | collective-permute-done | bytes 131104 | tf_op jit(solution)/shard_map/while/body/eval_jaxpr/ppermute | solution.py:19
  489.1 1.9 collective-permute-start.1
  491.0 39.2 %collective-permute-done.1 = bf16[2,64,512]{2,1,0:T(8,128)(2,1)S(1)} collective-permute-done((bf16[2,64,512]{2,1,0:T(8,128)(2,1)}, bf16[2,64,512]{2,1,0:T(8,128)(2,1)S(1)}, u32[]{:S(2)}, u32[]{:S(2)}) %collective-permute-start.1) | collective-permute-done | bytes 131104 | tf_op jit(solution)/shard_map/while/body/eval_jaxpr/ppermute | solution.py:19
  530.2 12.2 %conditional.9 = (bf16[2,64,512]{2,1,0:T(8,128)(2,1)}, f32[512,2048]{1,0:T(8,128)}) conditional(s32[]{:T(128)} %convert_element_type.340, f32[512,2048]{1,0:T(8,128)} %get-tuple-element.1233, (s32[]{:T(128)}, s32[]{:T(128)}, bf16[2,2,64,512]{3,2,1,0:T(8,128)(2,1)}, bf16[2,64,512]{2,1,0:T(8,128)(2,1)S(1)}, f32[2,64,1]{1,2,0:T(1,128)S(1)}, ...), branch_computations={%region_15.15_spmd, %region_16.21_spmd} | conditional | flops 946143296 | bytes 89922296 | solution.py:198
  537.7 1.4 copy-done.4
  540.5 2.0 copy-done.5
  542.5 1.9 collective-permute-start.1
  544.4 16.1 %collective-permute-done.1 = bf16[2,64,512]{2,1,0:T(8,128)(2,1)S(1)} collective-permute-done((bf16[2,64,512]{2,1,0:T(8,128)(2,1)}, bf16[2,64,512]{2,1,0:T(8,128)(2,1)S(1)}, u32[]{:S(2)}, u32[]{:S(2)}) %collective-permute-start.1) | collective-permute-done | bytes 131104 | tf_op jit(solution)/shard_map/while/body/eval_jaxpr/ppermute | solution.py:19
  560.5 12.2 %conditional.9 = (bf16[2,64,512]{2,1,0:T(8,128)(2,1)}, f32[512,2048]{1,0:T(8,128)}) conditional(s32[]{:T(128)} %convert_element_type.340, f32[512,2048]{1,0:T(8,128)} %get-tuple-element.1233, (s32[]{:T(128)}, s32[]{:T(128)}, bf16[2,2,64,512]{3,2,1,0:T(8,128)(2,1)}, bf16[2,64,512]{2,1,0:T(8,128)(2,1)S(1)}, f32[2,64,1]{1,2,0:T(1,128)S(1)}, ...), branch_computations={%region_15.15_spmd, %region_16.21_spmd} | conditional | flops 946143296 | bytes 89922296 | solution.py:198
  570.7 2.0 copy-done.5
  572.7 1.9 collective-permute-start.1
  574.6 5.1 collective-permute-done.1
  579.8 460.1 %reduce-scatter.2.cloned.1.call-done = f32[8,2048]{1,0:T(8,128)} async-done(((f32[512,2048]{1,0:T(8,128)}), f32[8,2048]{1,0:T(8,128)}) %reduce-scatter.2.cloned.1.call-update) | async-done | bytes 65552 | tf_op jit(solution)/shard_map/reduce_scatter | solution.py:210
  1039.8 1.5 fusion.159
  (154 shorter events, 52.0 us)
Async XLA Ops:
  6.5 128.2 %all-gather.3.cloned.1.call-start = ((), (), s32[]{:S(2)}) async-start(), calls=%async_computation.1 | async-start | bytes 2129920 | tf_op jit(solution)/shard_map/all_gather | solution.py:103
  7.3 246.1 %all-gather.5.cloned.1.call-start = ((), (), s32[]{:S(2)}) async-start(), calls=%async_computation.2 | async-start | bytes 2129920 | tf_op jit(solution)/shard_map/all_gather | solution.py:104
  8.0 1031.8 %reduce-scatter.2.cloned.1.call-start = ((), (), s32[]{:S(2)}) async-start(), calls=%async_computation.3 | async-start | bytes 4259840 | tf_op jit(solution)/shard_map/reduce_scatter | solution.py:210
  253.4 2.8 copy-start
  256.9 13.9 %collective-permute-start = (bf16[2,64,512]{2,1,0:T(8,128)(2,1)}, bf16[2,64,512]{2,1,0:T(8,128)(2,1)S(1)}, u32[]{:S(2)}, u32[]{:S(2)}) collective-permute-start(bf16[2,64,512]{2,1,0:T(8,128)(2,1)} %get-tuple-element.1100), channel_id=1, source_target_pairs={{0,64},{64,128},{128,192},{192,256},{256,320},{320,384},{384,448},... | collective-permute-start | bytes 393224 | tf_op jit(solution)/shard_map/while/body/eval_jaxpr/ppermute | solution.py:19
  270.9 3.7 copy-start.1
  274.5 0.9 copy-start.21
  274.6 1.4 copy-start.14
  275.1 1.6 copy-start.6
  275.1 1.9 copy-start.9
  276.1 2.0 copy-start.15
  277.5 1.2 copy-start.10
  277.5 1.2 copy-start.17
  279.5 7.2 collective-permute-start
  286.7 3.7 copy-start.1
  290.4 0.9 copy-start.21
  290.4 1.4 copy-start.14
  291.0 1.6 copy-start.6
  291.0 1.9 copy-start.9
  291.9 2.0 copy-start.15
  293.4 1.2 copy-start.10
  293.4 1.2 copy-start.17
  295.4 7.1 collective-permute-start
  303.1 13.0 %collective-permute-start = (bf16[2,64,512]{2,1,0:T(8,128)(2,1)}, bf16[2,64,512]{2,1,0:T(8,128)(2,1)S(1)}, u32[]{:S(2)}, u32[]{:S(2)}) collective-permute-start(bf16[2,64,512]{2,1,0:T(8,128)(2,1)} %get-tuple-element.1100), channel_id=1, source_target_pairs={{0,64},{64,128},{128,192},{192,256},{256,320},{320,384},{384,448},... | collective-permute-start | bytes 393224 | tf_op jit(solution)/shard_map/while/body/eval_jaxpr/ppermute | solution.py:19
  316.7 11.0 %collective-permute-start = (bf16[2,64,512]{2,1,0:T(8,128)(2,1)}, bf16[2,64,512]{2,1,0:T(8,128)(2,1)S(1)}, u32[]{:S(2)}, u32[]{:S(2)}) collective-permute-start(bf16[2,64,512]{2,1,0:T(8,128)(2,1)} %get-tuple-element.1100), channel_id=1, source_target_pairs={{0,64},{64,128},{128,192},{192,256},{256,320},{320,384},{384,448},... | collective-permute-start | bytes 393224 | tf_op jit(solution)/shard_map/while/body/eval_jaxpr/ppermute | solution.py:19
  328.4 17.9 %collective-permute-start = (bf16[2,64,512]{2,1,0:T(8,128)(2,1)}, bf16[2,64,512]{2,1,0:T(8,128)(2,1)S(1)}, u32[]{:S(2)}, u32[]{:S(2)}) collective-permute-start(bf16[2,64,512]{2,1,0:T(8,128)(2,1)} %get-tuple-element.1100), channel_id=1, source_target_pairs={{0,64},{64,128},{128,192},{192,256},{256,320},{320,384},{384,448},... | collective-permute-start | bytes 393224 | tf_op jit(solution)/shard_map/while/body/eval_jaxpr/ppermute | solution.py:19
  347.0 18.0 %collective-permute-start = (bf16[2,64,512]{2,1,0:T(8,128)(2,1)}, bf16[2,64,512]{2,1,0:T(8,128)(2,1)S(1)}, u32[]{:S(2)}, u32[]{:S(2)}) collective-permute-start(bf16[2,64,512]{2,1,0:T(8,128)(2,1)} %get-tuple-element.1100), channel_id=1, source_target_pairs={{0,64},{64,128},{128,192},{192,256},{256,320},{320,384},{384,448},... | collective-permute-start | bytes 393224 | tf_op jit(solution)/shard_map/while/body/eval_jaxpr/ppermute | solution.py:19
  365.6 25.9 %collective-permute-start = (bf16[2,64,512]{2,1,0:T(8,128)(2,1)}, bf16[2,64,512]{2,1,0:T(8,128)(2,1)S(1)}, u32[]{:S(2)}, u32[]{:S(2)}) collective-permute-start(bf16[2,64,512]{2,1,0:T(8,128)(2,1)} %get-tuple-element.1100), channel_id=1, source_target_pairs={{0,64},{64,128},{128,192},{192,256},{256,320},{320,384},{384,448},... | collective-permute-start | bytes 393224 | tf_op jit(solution)/shard_map/while/body/eval_jaxpr/ppermute | solution.py:19
  394.8 18.3 %collective-permute-start.1 = (bf16[2,64,512]{2,1,0:T(8,128)(2,1)}, bf16[2,64,512]{2,1,0:T(8,128)(2,1)S(1)}, u32[]{:S(2)}, u32[]{:S(2)}) collective-permute-start(bf16[2,64,512]{2,1,0:T(8,128)(2,1)} %get-tuple-element.1123), channel_id=1, source_target_pairs={{64,0},{128,64},{192,128},{256,192},{320,256},{384,320},{448,384},... | collective-permute-start | bytes 393224 | tf_op jit(solution)/shard_map/while/body/eval_jaxpr/ppermute | solution.py:19
  413.8 18.3 %collective-permute-start.1 = (bf16[2,64,512]{2,1,0:T(8,128)(2,1)}, bf16[2,64,512]{2,1,0:T(8,128)(2,1)S(1)}, u32[]{:S(2)}, u32[]{:S(2)}) collective-permute-start(bf16[2,64,512]{2,1,0:T(8,128)(2,1)} %get-tuple-element.1123), channel_id=1, source_target_pairs={{64,0},{128,64},{192,128},{256,192},{320,256},{384,320},{448,384},... | collective-permute-start | bytes 393224 | tf_op jit(solution)/shard_map/while/body/eval_jaxpr/ppermute | solution.py:19
  432.7 18.4 %collective-permute-start.1 = (bf16[2,64,512]{2,1,0:T(8,128)(2,1)}, bf16[2,64,512]{2,1,0:T(8,128)(2,1)S(1)}, u32[]{:S(2)}, u32[]{:S(2)}) collective-permute-start(bf16[2,64,512]{2,1,0:T(8,128)(2,1)} %get-tuple-element.1123), channel_id=1, source_target_pairs={{64,0},{128,64},{192,128},{256,192},{320,256},{384,320},{448,384},... | collective-permute-start | bytes 393224 | tf_op jit(solution)/shard_map/while/body/eval_jaxpr/ppermute | solution.py:19
  451.8 18.0 %collective-permute-start.1 = (bf16[2,64,512]{2,1,0:T(8,128)(2,1)}, bf16[2,64,512]{2,1,0:T(8,128)(2,1)S(1)}, u32[]{:S(2)}, u32[]{:S(2)}) collective-permute-start(bf16[2,64,512]{2,1,0:T(8,128)(2,1)} %get-tuple-element.1123), channel_id=1, source_target_pairs={{64,0},{128,64},{192,128},{256,192},{320,256},{384,320},{448,384},... | collective-permute-start | bytes 393224 | tf_op jit(solution)/shard_map/while/body/eval_jaxpr/ppermute | solution.py:19
  470.5 18.0 %collective-permute-start.1 = (bf16[2,64,512]{2,1,0:T(8,128)(2,1)}, bf16[2,64,512]{2,1,0:T(8,128)(2,1)S(1)}, u32[]{:S(2)}, u32[]{:S(2)}) collective-permute-start(bf16[2,64,512]{2,1,0:T(8,128)(2,1)} %get-tuple-element.1123), channel_id=1, source_target_pairs={{64,0},{128,64},{192,128},{256,192},{320,256},{384,320},{448,384},... | collective-permute-start | bytes 393224 | tf_op jit(solution)/shard_map/while/body/eval_jaxpr/ppermute | solution.py:19
  489.1 41.1 %collective-permute-start.1 = (bf16[2,64,512]{2,1,0:T(8,128)(2,1)}, bf16[2,64,512]{2,1,0:T(8,128)(2,1)S(1)}, u32[]{:S(2)}, u32[]{:S(2)}) collective-permute-start(bf16[2,64,512]{2,1,0:T(8,128)(2,1)} %get-tuple-element.1123), channel_id=1, source_target_pairs={{64,0},{128,64},{192,128},{256,192},{320,256},{384,320},{448,384},... | collective-permute-start | bytes 393224 | tf_op jit(solution)/shard_map/while/body/eval_jaxpr/ppermute | solution.py:19
  530.2 1.8 copy-start.13
  532.0 1.6 copy-start.3
  533.6 1.6 copy-start.8
  533.6 1.6 copy-start.16
  537.0 2.2 copy-start.4
  540.4 2.0 copy-start.5
  542.5 18.0 %collective-permute-start.1 = (bf16[2,64,512]{2,1,0:T(8,128)(2,1)}, bf16[2,64,512]{2,1,0:T(8,128)(2,1)S(1)}, u32[]{:S(2)}, u32[]{:S(2)}) collective-permute-start(bf16[2,64,512]{2,1,0:T(8,128)(2,1)} %get-tuple-element.1123), channel_id=1, source_target_pairs={{64,0},{128,64},{192,128},{256,192},{320,256},{384,320},{448,384},... | collective-permute-start | bytes 393224 | tf_op jit(solution)/shard_map/while/body/eval_jaxpr/ppermute | solution.py:19
  560.5 1.8 copy-start.13
  562.2 1.6 copy-start.3
  563.8 1.6 copy-start.8
  563.8 1.6 copy-start.16
  567.2 2.2 copy-start.4
  570.7 2.0 copy-start.5
  572.7 7.1 collective-permute-start.1
  (2 other events, 1.4 us)
Sparse Core Ops, SparseCore 0:
  9.5 125.1 all-gather.2
  136.8 116.4 all-gather.4
  579.9 459.9 reduce-scatter.1
where the time goes:
time: 1050 us
  waiting for transfers between devices  883 us (84%)
  starting transfers between devices  94.5 us (9%)
  local copies, waits for them, and re-layouts  26 us (2%)
  matrix products  20.2 us (2%)
  between operations  13.2 us (1%)
    reduce_scatter x1, waiting for transfers between devices, shards(): lax.psum_scatter(curvature_state, 'dp', scatter_dimension=0, tiled=True)  460 us
    ppermute x16, waiting for transfers between devices, passed_along(): return lax.ppermute(value, axis, pairs)  177 us
    all_gather x1, waiting for transfers between devices, shards(): lax.all_gather(w_in, 'dp', axis=1, tiled=True)  127 us
    all_gather x1, waiting for transfers between devices, shards(): lax.all_gather(w_out, 'dp', axis=1, tiled=True)  119 us
    ppermute x16, starting transfers between devices, passed_along(): return lax.ppermute(value, axis, pairs)  94.4 us
  transfers between devices with their start and end apart: 19, of which 19 were waited for; matrix products, arithmetic and copies ran while one was open for 0% of the time, Pallas kernels for 0%

commit v1 on v0

v1 whole, which is shorter than its diff:
```python
import functools
import itertools

import jax
import jax.numpy as jnp
from jax import lax
from jax.experimental import pallas as pl
from jax.experimental.pallas import tpu as pltpu
from jax.sharding import Mesh, PartitionSpec as P

EPSILON = 1e-05
SQRT_HALF = 0.7071067811865476
INV_ROOT_TWO_PI = 0.3989422804014327
CONTRACT_LAST = (((1,), (1,)), ((), ()))
CONTRACT_FIRST = (((0,), (0,)), ((), ()))

NAMES = ("zh", "x", "b4", "b2", "b1", "y", "c")
SIZES = (2, 4, 2, 2, 2, 4, 2)
SECTION = ("zh", "x")
DP = ("b4", "b2", "b1", "y", "c")
LAYERS = 8
FEATURES = 512
HIDDEN = 2048
ROWS = 128
TOKENS = 8192
CHUNK = 512
CHUNKS = HIDDEN // CHUNK
VMEM_BYTES = 40 * 1024 * 1024
ANY = pl.BlockSpec(memory_space=pl.ANY)
SMEM = pl.BlockSpec(memory_space=pltpu.SMEM)


def flat(place):
    index = 0
    for size, at in zip(SIZES, place):
        index = index * size + at
    return index


def routed(value, route):
    pairs = []
    for place in itertools.product(*(range(size) for size in SIZES)):
        there = route(*place)
        if there is not None:
            pairs.append((flat(place), flat(there)))
    return lax.ppermute(value, NAMES, pairs)


def swap_b4(zh, x, b4, b2, b1, y, c):
    return (zh, x, 1 - b4, b2, b1, y, c)


def swap_b2(zh, x, b4, b2, b1, y, c):
    return (zh, x, b4, 1 - b2, b1, y, c)


def swap_b1(zh, x, b4, b2, b1, y, c):
    return (zh, x, b4, b2, 1 - b1, y, c)


def swap_even(zh, x, b4, b2, b1, y, c):
    return (zh, x, b4, b2, b1, y ^ 1, c)


def swap_odd(zh, x, b4, b2, b1, y, c):
    return (zh, x, b4, b2, b1, y ^ 3, c)


def swap_core(zh, x, b4, b2, b1, y, c):
    return (zh, x, b4, b2, b1, y, 1 - c)


def up_from(section):
    def route(zh, x, b4, b2, b1, y, c):
        if zh * 4 + x != section:
            return None
        if x == 3:
            return (zh + 1, 0, 1 - b4, b2, b1, y, c)
        return (zh, x + 1, b4, b2, b1, y, c)

    return route


def down_from(section):
    def route(zh, x, b4, b2, b1, y, c):
        if zh * 4 + x != section:
            return None
        if x == 0:
            return (zh - 1, 3, 1 - b4, b2, b1, y, c)
        return (zh, x - 1, b4, b2, b1, y, c)

    return route


def merged(own, other, bit):
    first = bit == 0
    return jnp.concatenate([jnp.where(first, own, other), jnp.where(first, other, own)], axis=0)


def gathered(block):
    block = merged(block, routed(block, swap_b4), lax.axis_index("b4"))
    block = merged(block, routed(block, swap_b2), lax.axis_index("b2"))
    block = merged(block, routed(block, swap_b1), lax.axis_index("b1"))
    rows, half = block.shape[0], block.shape[1] // 2
    y = lax.axis_index("y")
    left, right = block[:, :half], block[:, half:]
    left_two = merged(left, routed(left, swap_even), y % 2)
    right_two = merged(right, routed(right, swap_odd), y // 2)
    left_four = merged(left_two, routed(left_two, swap_odd), y // 2)
    other = routed(right_two, swap_even)
    outer = (y == 0) | (y == 3)
    own_a, own_b, oth_a, oth_b = right_two[:rows], right_two[rows:], other[:rows], other[rows:]
    right_four = jnp.concatenate(
        [
            jnp.where(outer, own_a, oth_a),
            jnp.where(outer, oth_a, own_a),
            jnp.where(outer, oth_b, own_b),
            jnp.where(outer, own_b, oth_b),
        ],
        axis=0,
    )
    core = lax.axis_index("c")
    return jnp.concatenate(
        [
            merged(left_four, routed(left_four, swap_core), core),
            merged(right_four, routed(right_four, swap_core), core),
        ],
        axis=1,
    )


def feature_order():
    position = lax.broadcasted_iota(jnp.int32, (FEATURES, FEATURES), 1)
    natural = lax.broadcasted_iota(jnp.int32, (FEATURES, FEATURES), 0)
    core, y = position // 256, (position // 64) % 4
    b1, b2, b4, row = (position // 32) % 2, (position // 16) % 2, (position // 8) % 2, position % 8
    return (natural == (b4 * 4 + b2 * 2 + b1) * 64 + y * 16 + core * 8 + row).astype(jnp.bfloat16)


def row_mean(values):
    return jnp.mean(values, axis=-1, keepdims=True)


def copies(pairs, sem):
    return [pltpu.make_async_copy(src, dst, sem.at[i]) for i, (src, dst) in enumerate(pairs)]


def columns(ref, chunk):
    return ref.at[:, pl.ds(pl.multiple_of(chunk * CHUNK, CHUNK), CHUNK)]


def lines(ref, chunk):
    return ref.at[pl.ds(pl.multiple_of(chunk * CHUNK, CHUNK), CHUNK), :]


def forward_kernel(tick, *refs):
    last, first = tick == LAYERS - 1, tick == 0
    section, pair_in, w_in, probe, w_out = refs[:5]
    refs = refs[5:]
    if last:
        goal, refs = refs[0], refs[1:]
    if not first:
        refs = refs[3:]
    pair_out, norm_out, stat_out, slope_out = refs[:4]
    refs = refs[4:]
    pair_v, in_v, probe_v, out_v, norm_v, stat_v, slope_v, lhs_v, acc_v, send_v, goal_v = refs[:11]
    head_sem, weight_sem, store_sem = refs[11:]

    @pl.when(section[0] == tick)
    def _():
        def weights(chunk):
            return [
                pltpu.make_async_copy(columns(w_in, chunk), in_v.at[chunk], weight_sem.at[0, chunk]),
                pltpu.make_async_copy(columns(probe, chunk), probe_v.at[chunk], weight_sem.at[1, chunk]),
                pltpu.make_async_copy(lines(w_out, chunk), out_v.at[chunk], weight_sem.at[2, chunk]),
            ]

        head = [pltpu.make_async_copy(pair_in, pair_v, head_sem.at[0])]
        if last:
            head.append(pltpu.make_async_copy(goal, goal_v, head_sem.at[1]))
        for copy in head:
            copy.start()
        for chunk in range(CHUNKS):
            for copy in weights(chunk):
                copy.start()
        for copy in head:
            copy.wait()
        inflow = pair_v[0].astype(jnp.float32)
        inflow_t = pair_v[1].astype(jnp.float32)
        centred = inflow - row_mean(inflow)
        rscale = lax.rsqrt(row_mean(centred * centred) + EPSILON)
        normed = centred * rscale
        tangent_dot = row_mean(normed * inflow_t)
        normed_t = rscale * (inflow_t - row_mean(inflow_t) - normed * tangent_dot)
        norm_v[0] = normed
        norm_v[1] = normed_t
        stat_v[0] = jnp.broadcast_to(rscale, (ROWS, 128))
        stat_v[1] = jnp.broadcast_to(tangent_dot, (ROWS, 128))
        lhs_v[:ROWS] = normed.astype(jnp.bfloat16)
        lhs_v[ROWS:] = normed_t.astype(jnp.bfloat16)
        acc_v[:ROWS] = inflow
        acc_v[ROWS:] = inflow_t
        stores = [
            pltpu.make_async_copy(norm_v, norm_out, head_sem.at[2]),
            pltpu.make_async_copy(stat_v, stat_out, head_sem.at[3]),
        ]
        for copy in stores:
            copy.start()

        def slopes(chunk):
            return pltpu.make_async_copy(slope_v.at[chunk], slope_out.at[chunk], store_sem.at[chunk])

        def step(chunk, carry):
            for copy in weights(chunk):
                copy.wait()
            both = jnp.dot(lhs_v[...], in_v[chunk], preferred_element_type=jnp.float32)
            preact = both[:ROWS]
            preact_t = both[ROWS:] + jnp.dot(lhs_v[:ROWS], probe_v[chunk], preferred_element_type=jnp.float32)
            normal_cdf = 0.5 * (1.0 + lax.erf(preact * SQRT_HALF))
            density = INV_ROOT_TWO_PI * jnp.exp(-0.5 * preact * preact)
            slope = normal_cdf + preact * density
            slope_v[chunk, 0] = slope
            slope_v[chunk, 1] = density * (2.0 - preact * preact) * preact_t
            slopes(chunk).start()
            hidden = jnp.concatenate([preact * normal_cdf, slope * preact_t], axis=0).astype(jnp.bfloat16)
            acc_v[...] += jnp.dot(hidden, out_v[chunk], preferred_element_type=jnp.float32)
            return carry

        lax.fori_loop(0, CHUNKS, step, 0)
        if last:
            send_v[0] = ((acc_v[:ROWS] - goal_v[...].astype(jnp.float32)) / TOKENS).astype(jnp.bfloat16)
            send_v[1] = (acc_v[ROWS:] / TOKENS).astype(jnp.bfloat16)
        else:
            send_v[0] = acc_v[:ROWS].astype(jnp.bfloat16)
            send_v[1] = acc_v[ROWS:].astype(jnp.bfloat16)
        send = pltpu.make_async_copy(send_v, pair_out, head_sem.at[4])
        send.start()
        for copy in stores:
            copy.wait()
        for chunk in range(CHUNKS):
            slopes(chunk).wait()
        send.wait()


NORM = jax.ShapeDtypeStruct((2, ROWS, FEATURES), jnp.float32)
STAT = jax.ShapeDtypeStruct((2, ROWS, 128), jnp.float32)
SLOPE = jax.ShapeDtypeStruct((CHUNKS, 2, ROWS, CHUNK), jnp.float32)
PAIR = jax.ShapeDtypeStruct((2, ROWS, FEATURES), jnp.bfloat16)
GRADS = jax.ShapeDtypeStruct((CHUNKS, 2 * ROWS, CHUNK), jnp.bfloat16)


def vmem(struct):
    return pltpu.VMEM(struct.shape, struct.dtype)


WEIGHT = pltpu.VMEM((CHUNKS, FEATURES, CHUNK), jnp.bfloat16)


def forward_call(tick, section, pair, w_in, probe, w_out, goal, kept):
    last = tick == LAYERS - 1
    operands = [section, pair, w_in, probe, w_out] + ([goal] if last else []) + list(kept)
    start = len(operands) - len(kept)
    aliases = {start + i: 1 + i for i in range(len(kept))}
    return pl.pallas_call(
        functools.partial(forward_kernel, tick),
        out_shape=[PAIR, NORM, STAT, SLOPE],
        in_specs=[SMEM] + [ANY] * (len(operands) - 1),
        out_specs=[ANY] * 4,
        scratch_shapes=[
            vmem(PAIR),
            WEIGHT,
            WEIGHT,
            WEIGHT,
            vmem(NORM),
            vmem(STAT),
            vmem(SLOPE),
            pltpu.VMEM((2 * ROWS, FEATURES), jnp.bfloat16),
            pltpu.VMEM((2 * ROWS, FEATURES), jnp.float32),
            vmem(PAIR),
            pltpu.VMEM((ROWS, FEATURES), jnp.bfloat16),
            pltpu.SemaphoreType.DMA((5,)),
            pltpu.SemaphoreType.DMA((3, CHUNKS)),
            pltpu.SemaphoreType.DMA((CHUNKS,)),
        ],
        input_output_aliases=aliases,
        compiler_params=pltpu.CompilerParams(vmem_limit_bytes=VMEM_BYTES),
        name=f"layer_up_{tick}",
    )(*operands)


def hidden_grads(pair_v, out_chunk, slope_chunk, curve_chunk):
    both = lax.dot_general(pair_v, out_chunk, CONTRACT_LAST, preferred_element_type=jnp.float32)
    grad_hidden, grad_hidden_t = both[:ROWS], both[ROWS:]
    grad_pre = grad_hidden * slope_chunk
    grad_pre_t = grad_hidden_t * slope_chunk + grad_hidden * curve_chunk
    return grad_pre.astype(jnp.bfloat16), grad_pre_t.astype(jnp.bfloat16)


def norm_apply(values, normed, rscale):
    return rscale * (values - row_mean(values) - normed * row_mean(normed * values))


def backward_kernel(tick, *refs):
    section, pair_in, w_in, probe, w_out, norm, stat, slope = refs[:8]
    refs = refs[8:] if tick == 0 else refs[9:]
    pair_out, grads_out = refs[:2]
    pair_v, in_v, probe_v, out_v, norm_v, stat_v, slope_v, grads_v, acc_v, acc_t_v, send_v = refs[2:13]
    head_sem, weight_sem, store_sem = refs[13:]

    @pl.when(section[0] == LAYERS - 1 - tick)
    def _():
        def weights(chunk):
            return [
                pltpu.make_async_copy(lines(w_out, chunk), out_v.at[chunk], weight_sem.at[0, chunk]),
                pltpu.make_async_copy(slope.at[chunk], slope_v.at[chunk], weight_sem.at[1, chunk]),
                pltpu.make_async_copy(columns(w_in, chunk), in_v.at[chunk], weight_sem.at[2, chunk]),
                pltpu.make_async_copy(columns(probe, chunk), probe_v.at[chunk], weight_sem.at[3, chunk]),
            ]

        head = pltpu.make_async_copy(pair_in, pair_v, head_sem.at[0])
        head.start()
        for chunk in range(CHUNKS):
            for copy in weights(chunk):
                copy.start()
        tail = [
            pltpu.make_async_copy(norm, norm_v, head_sem.at[1]),
            pltpu.make_async_copy(stat, stat_v, head_sem.at[2]),
        ]
        for copy in tail:
            copy.start()
        acc_v[...] = jnp.zeros_like(acc_v)
        acc_t_v[...] = jnp.zeros_like(acc_t_v)
        head.wait()

        def grads(chunk):
            return pltpu.make_async_copy(grads_v.at[chunk], grads_out.at[chunk], store_sem.at[chunk])

        def step(chunk, carry):
            for copy in weights(chunk):
                copy.wait()
            low_grad, low_grad_t = hidden_grads(
                pair_v[...].reshape(2 * ROWS, FEATURES), out_v[chunk], slope_v[chunk, 0], slope_v[chunk, 1]
            )
            grads_v[chunk, :ROWS] = low_grad_t
            grads_v[chunk, ROWS:] = low_grad
            grads(chunk).start()
            both = jnp.concatenate([low_grad_t, low_grad], axis=0)
            acc_v[...] += lax.dot_general(both, in_v[chunk], CONTRACT_LAST, preferred_element_type=jnp.float32)
            acc_t_v[...] += lax.dot_general(
                low_grad, probe_v[chunk], CONTRACT_LAST, preferred_element_type=jnp.float32
            )
            return carry

        lax.fori_loop(0, CHUNKS, step, 0)
        for copy in tail:
            copy.wait()
        normed, normed_t = norm_v[0], norm_v[1]
        rscale, tangent_dot = stat_v[0][:, :1], stat_v[1][:, :1]
        grad_norm = acc_v[ROWS:]
        grad_norm_t = acc_v[:ROWS] + acc_t_v[...]
        through = norm_apply(grad_norm, normed, rscale)
        through_t = (
            norm_apply(grad_norm_t, normed, rscale)
            - rscale * tangent_dot * through
            - rscale * (normed_t * row_mean(normed * grad_norm) + normed * row_mean(normed_t * grad_norm))
        )
        send_v[0] = (pair_v[0].astype(jnp.float32) + through).astype(jnp.bfloat16)
        send_v[1] = (pair_v[1].astype(jnp.float32) + through_t).astype(jnp.bfloat16)
        send = pltpu.make_async_copy(send_v, pair_out, head_sem.at[3])
        send.start()
        for chunk in range(CHUNKS):
            grads(chunk).wait()
        send.wait()


def backward_call(tick, section, pair, w_in, probe, w_out, kept, grads):
    operands = [section, pair, w_in, probe, w_out, *kept, *grads]
    return pl.pallas_call(
        functools.partial(backward_kernel, tick),
        out_shape=[PAIR, GRADS],
        in_specs=[SMEM] + [ANY] * (len(operands) - 1),
        out_specs=[ANY] * 2,
        scratch_shapes=[
            vmem(PAIR),
            WEIGHT,
            WEIGHT,
            WEIGHT,
            vmem(NORM),
            vmem(STAT),
            vmem(SLOPE),
            vmem(GRADS),
            pltpu.VMEM((2 * ROWS, FEATURES), jnp.float32),
            pltpu.VMEM((ROWS, FEATURES), jnp.float32),
            vmem(PAIR),
            pltpu.SemaphoreType.DMA((4,)),
            pltpu.SemaphoreType.DMA((4, CHUNKS)),
            pltpu.SemaphoreType.DMA((CHUNKS,)),
        ],
        input_output_aliases={8: 1} if grads else {},
        compiler_params=pltpu.CompilerParams(vmem_limit_bytes=VMEM_BYTES),
        name=f"layer_down_{tick}",
    )(*operands)


def curvature_kernel(*refs):
    section, core, pair_in, w_out, norm, slope, grads, away_out, stay_out = refs[:9]
    pair_v, out_v, norm_v, slope_v, grads_v, half_v, away_v, stay_v = refs[9:17]
    head_sem, weight_sem, store_sem = refs[17:]
    bottom = section[0] == 0
    load_norm = pltpu.make_async_copy(norm, norm_v, head_sem.at[0])
    load_norm.start()

    @pl.when(bottom)
    def _():
        load_pair = pltpu.make_async_copy(pair_in, pair_v, head_sem.at[1])
        load_pair.start()

        def weights(chunk):
            return [
                pltpu.make_async_copy(lines(w_out, chunk), out_v.at[chunk], weight_sem.at[0, chunk]),
                pltpu.make_async_copy(slope.at[chunk], slope_v.at[chunk], weight_sem.at[1, chunk]),
            ]

        for chunk in range(CHUNKS):
            for copy in weights(chunk):
                copy.start()
        load_pair.wait()

        def step(chunk, carry):
            for copy in weights(chunk):
                copy.wait()
            low_grad, low_grad_t = hidden_grads(
                pair_v[...].reshape(2 * ROWS, FEATURES), out_v[chunk], slope_v[chunk, 0], slope_v[chunk, 1]
            )
            grads_v[chunk, :ROWS] = low_grad_t
            grads_v[chunk, ROWS:] = low_grad
            return carry

        lax.fori_loop(0, CHUNKS, step, 0)

    @pl.when(jnp.logical_not(bottom))
    def _():
        load_grads = pltpu.make_async_copy(grads, grads_v, head_sem.at[2])
        load_grads.start()
        load_grads.wait()

    load_norm.wait()
    for half in range(2):
        for which in range(2):
            half_v[half, which * ROWS : (which + 1) * ROWS] = norm_v[which, :, half * 256 : (half + 1) * 256].astype(
                jnp.bfloat16
            )
    own = core[0]

    def away(chunk):
        return pltpu.make_async_copy(away_v.at[chunk], columns(away_out, chunk), store_sem.at[0, chunk])

    def stay(chunk):
        return pltpu.make_async_copy(stay_v.at[chunk], columns(stay_out, chunk), store_sem.at[1, chunk])

    def step(chunk, carry):
        away_v[chunk] = lax.dot_general(
            half_v[1 - own], grads_v[chunk], CONTRACT_FIRST, preferred_element_type=jnp.float32
        ).astype(jnp.bfloat16)
        away(chunk).start()
        stay_v[chunk] = lax.dot_general(half_v[own], grads_v[chunk], CONTRACT_FIRST, preferred_element_type=jnp.float32)
        stay(chunk).start()
        return carry

    lax.fori_loop(0, CHUNKS, step, 0)
    for chunk in range(CHUNKS):
        away(chunk).wait()
        stay(chunk).wait()


def curvature_call(section, core, pair, w_out, norm, slope, grads):
    half = FEATURES // 2
    return pl.pallas_call(
        curvature_kernel,
        out_shape=[
            jax.ShapeDtypeStruct((half, HIDDEN), jnp.bfloat16),
            jax.ShapeDtypeStruct((half, HIDDEN), jnp.float32),
        ],
        in_specs=[SMEM, SMEM] + [ANY] * 5,
        out_specs=[ANY] * 2,
        scratch_shapes=[
            vmem(PAIR),
            WEIGHT,
            vmem(NORM),
            vmem(SLOPE),
            vmem(GRADS),
            pltpu.VMEM((2, 2 * ROWS, half), jnp.bfloat16),
            pltpu.VMEM((CHUNKS, half, CHUNK), jnp.bfloat16),
            pltpu.VMEM((CHUNKS, half, CHUNK), jnp.float32),
            pltpu.SemaphoreType.DMA((3,)),
            pltpu.SemaphoreType.DMA((2, CHUNKS)),
            pltpu.SemaphoreType.DMA((2, CHUNKS)),
        ],
        compiler_params=pltpu.CompilerParams(vmem_limit_bytes=VMEM_BYTES),
        name="layer_curvature",
    )(section, core, pair, w_out, norm, slope, grads)


def shards(inputs, targets, w_in, w_out, probes):
    section = jnp.reshape(lax.axis_index(SECTION), (1,)).astype(jnp.int32)
    core = jnp.reshape(lax.axis_index("c"), (1,)).astype(jnp.int32)
    order = feature_order()
    full_in = gathered(w_in[0])
    full_out = gathered(jnp.dot(w_out[0], order))
    full_out = (
        full_out.reshape(2, 4, 2, 2, 2, 32, FEATURES).transpose(4, 3, 2, 1, 0, 5, 6).reshape(HIDDEN, FEATURES)
    )
    probe = lax.dot_general(order, probes[0], CONTRACT_FIRST, preferred_element_type=jnp.bfloat16)
    fresh = jnp.dot(inputs, order)
    goal = jnp.dot(routed(targets, swap_b4), order)
    pair = jnp.stack([fresh, jnp.zeros_like(fresh)])
    kept = ()
    for tick in range(LAYERS):
        pair, *kept = forward_call(tick, section, pair, full_in, probe, full_out, goal, kept)
        if tick < LAYERS - 1:
            pair = routed(pair, up_from(tick))
    grads = ()
    for tick in range(LAYERS - 1):
        pair, *grads = backward_call(tick, section, pair, full_in, probe, full_out, kept, grads)
        pair = routed(pair, down_from(LAYERS - 1 - tick))
    away, stay = curvature_call(section, core, pair, full_out, kept[0], kept[2], grads[0])
    summed = (stay + routed(away, swap_core).astype(jnp.float32)).astype(jnp.bfloat16)
    summed = lax.all_to_all(summed.reshape(4, 64, HIDDEN), "y", 0, 0, tiled=True)
    summed = jnp.sum(summed.astype(jnp.float32), axis=0).astype(jnp.bfloat16)
    summed = lax.all_to_all(summed.reshape(8, 8, HIDDEN), ("b1", "b2", "b4"), 0, 0, tiled=True)
    summed = jnp.sum(summed.astype(jnp.float32), axis=0)
    probe_own = lax.dynamic_slice_in_dim(probes[0], lax.axis_index(DP) * 8, 8, 0)
    return (probe_own.astype(jnp.float32) * summed)[None]


def solution(mesh):
    fine = Mesh(mesh.devices.reshape(SIZES), NAMES)
    return jax.shard_map(
        shards,
        mesh=fine,
        in_specs=(
            P(DP, None),
            P(DP, None),
            P(SECTION, DP, None),
            P(SECTION, DP, None),
            P(SECTION, None, None),
        ),
        out_specs=P(SECTION, DP, None),
        check_vma=False,
    )
```

time: 1050 us -> 325 us (0.31)
  the two profiles are of different devices: /device:TPU:2 before, /device:TPU:8 now
where the time goes in v1:
time: 325 us; the launch traced here: 324 us
  waiting for transfers between devices  192 us (59%)
  starting transfers between devices  91.5 us (28%)
  blocking collectives  17.3 us (5%)
  Pallas kernels  12 us (4%)
  other arithmetic  5.11 us (2%)
  matrix products  4.45 us (1%)
    ppermute x34, waiting for transfers between devices, routed(): return lax.ppermute(value, NAMES, pairs)  176 us
    ppermute x34, starting transfers between devices, routed(): return lax.ppermute(value, NAMES, pairs)  79.6 us
    all_to_all x1, blocking collectives, shards(): lax.all_to_all(summed.reshape(4, 64, HIDDEN), 'y', 0, 0, tiled=True)  17.3 us
    all_to_all x1, waiting for transfers between devices, shards(): lax.all_to_all(summed.reshape(8, 8, HIDDEN), ('b1', 'b2', 'b4'), 0, 0, ti...  15.5 us
    all_to_all x1, starting transfers between devices, shards(): lax.all_to_all(summed.reshape(8, 8, HIDDEN), ('b1', 'b2', 'b4'), 0, 0, ti...  11.9 us
  transfers between devices with their start and end apart: 35, of which 9 were waited for; matrix products, arithmetic and copies ran while one was open for 2% of the time, Pallas kernels for 0%

profile of v1, /device:TPU:8, one launch (start us, length us, event | category | flops | bytes accessed | tf_op | source)
XLA Modules:
  0.0 323.7 jit_solution(557932685634318195)
XLA Ops:
  0.0 9.2 %collective-permute-start = (bf16[8,2048]{1,0:T(8,128)(2,1)}, bf16[8,2048]{1,0:T(8,128)(2,1)S(1)}, u32[]{:S(2)}, u32[]{:S(2)}) collective-permute-start(bf16[8,2048]{1,0:T(8,128)(2,1)} %bitcast.51), channel_id=1, source_target_pairs={{0,32},{1,33},{2,34},{3,35},{4,36},{5,37},{6,38},{7,39},{8,40},{9,... | collective-permute-start | bytes 98312 | tf_op jit(solution)/shard_map/ppermute | solution.py:46
  9.6 1.0 convolution_bitcast_fusion.2
  10.6 1.9 collective-permute-start.9
  12.5 2.9 fusion.refs_3_
  15.8 5.2 %collective-permute-start.1 = (bf16[16,2048]{1,0:T(8,128)(2,1)S(1)}, bf16[16,2048]{1,0:T(8,128)(2,1)S(1)}, u32[]{:S(2)}, u32[]{:S(2)}) collective-permute-start(bf16[16,2048]{1,0:T(8,128)(2,1)S(1)} %pad_maximum_fusion.12), channel_id=1, source_target_pairs={{0,16},{1,17},{2,18},{3,19},{4,20},{5,21},{6,22},{7,23},{8,24},{9,... | collective-permute-start | bytes 196616 | tf_op jit(solution)/shard_map/ppermute | solution.py:46
  21.1 4.8 %collective-permute-start.10 = (bf16[64,512]{1,0:T(8,128)(2,1)S(1)}, bf16[64,512]{1,0:T(8,128)(2,1)S(1)}, u32[]{:S(2)}, u32[]{:S(2)}) collective-permute-start(bf16[64,512]{1,0:T(8,128)(2,1)S(1)} %pad_maximum_fusion.13), channel_id=1, source_target_pairs={{0,16},{1,17},{2,18},{3,19},{4,20},{5,21},{6,22},{7,23},{8,24},{9,... | collective-permute-start | bytes 196616 | tf_op jit(solution)/shard_map/ppermute | solution.py:46
  26.0 3.4 %collective-permute-start.2 = (bf16[32,2048]{1,0:T(8,128)(2,1)S(1)}, bf16[32,2048]{1,0:T(8,128)(2,1)S(1)}, u32[]{:S(2)}, u32[]{:S(2)}) collective-permute-start(bf16[32,2048]{1,0:T(8,128)(2,1)S(1)} %pad_maximum_fusion.10), channel_id=1, source_target_pairs={{0,8},{1,9},{2,10},{3,11},{4,12},{5,13},{6,14},{7,15},{8,0},{9,1},... | collective-permute-start | bytes 393224 | tf_op jit(solution)/shard_map/ppermute | solution.py:46
  29.5 2.9 collective-permute-start.11
  32.4 1.5 collective-permute-done.2
  34.0 3.1 collective-permute-start.3
  37.1 3.6 %collective-permute-start.6 = (bf16[64,1024]{1,0:T(8,128)(2,1)S(1)}, bf16[64,1024]{1,0:T(8,128)(2,1)S(1)}, u32[]{:S(2)}, u32[]{:S(2)}) collective-permute-start(bf16[64,1024]{1,0:T(8,128)(2,1)S(1)} %get-tuple-element.134), channel_id=1, source_target_pairs={{0,6},{1,7},{2,4},{3,5},{4,2},{5,3},{6,0},{7,1},{8,14},{9,15},{10,... | collective-permute-start | bytes 393224 | tf_op jit(solution)/shard_map/ppermute | solution.py:46
  40.8 3.3 %collective-permute-start.12 = (bf16[256,256]{1,0:T(8,128)(2,1)S(1)}, bf16[256,256]{1,0:T(8,128)(2,1)S(1)}, u32[]{:S(2)}, u32[]{:S(2)}) collective-permute-start(bf16[256,256]{1,0:T(8,128)(2,1)S(1)} %get-tuple-element.123), channel_id=1, source_target_pairs={{0,2},{1,3},{2,0},{3,1},{4,6},{5,7},{6,4},{7,5},{8,10},{9,11},{10,... | collective-permute-start | bytes 393224 | tf_op jit(solution)/shard_map/ppermute | solution.py:46
  44.0 2.4 collective-permute-start.15
  46.5 3.5 %collective-permute-start.4 = (bf16[128,1024]{1,0:T(8,128)(2,1)S(1)}, bf16[128,1024]{1,0:T(8,128)(2,1)S(1)}, u32[]{:S(2)}, u32[]{:S(2)}) collective-permute-start(bf16[128,1024]{1,0:T(8,128)(2,1)S(1)} %pad_maximum_fusion.4), channel_id=1, source_target_pairs={{0,6},{1,7},{2,4},{3,5},{4,2},{5,3},{6,0},{7,1},{8,14},{9,15},{10,... | collective-permute-start | bytes 786440 | tf_op jit(solution)/shard_map/ppermute | solution.py:46
  50.0 3.8 %collective-permute-start.7 = (bf16[128,1024]{1,0:T(8,128)(2,1)S(1)}, bf16[128,1024]{1,0:T(8,128)(2,1)S(1)}, u32[]{:S(2)}, u32[]{:S(2)}) collective-permute-start(bf16[128,1024]{1,0:T(8,128)(2,1)S(1)} %pad_maximum_fusion.5), channel_id=1, source_target_pairs={{0,2},{1,3},{2,0},{3,1},{4,6},{5,7},{6,4},{7,5},{8,10},{9,11},{10,... | collective-permute-start | bytes 786440 | tf_op jit(solution)/shard_map/ppermute | solution.py:46
  53.9 2.3 collective-permute-start.13
  56.2 2.8 collective-permute-start.16
  59.2 1.9 collective-permute-start.5
  61.1 1.1 collective-permute-done.13
  62.3 1.9 collective-permute-start.14
  64.6 2.2 collective-permute-start.17
  66.9 2.2 collective-permute-start.8
  71.1 4.5 %layer_up_0.1 = (bf16[2,128,512]{2,1,0:T(8,128)(2,1)S(1)}, f32[2,128,512]{2,1,0:T(8,128)S(1)}, f32[2,128,128]{2,1,0:T(8,128)S(1)}, f32[4,2,128,512]{3,2,1,0:T(8,128)S(1)}) custom-call(s32[1]{0:T(128)} %bitcast.refs_0_, bf16[2,128,512]{2,1,0:T(8,128)(2,1)S(1)} %stack.7.refs_1_, bf16[512,2048]{1,0:T(8,128)(2,1)S(1)} %maximum_maximum_fusion.refs_2_, ...), custom_call_target="tpu_custom_call" | custom-call | tf_op jit(solution)/shard_map/layer_up_0/pallas_call | solution.py:264
  75.6 1.3 collective-permute-start.18
  76.9 6.2 %collective-permute-done.18.refs_1_ = bf16[2,128,512]{2,1,0:T(8,128)(2,1)S(1)} collective-permute-done((bf16[2,128,512]{2,1,0:T(8,128)(2,1)S(1)}, bf16[2,128,512]{2,1,0:T(8,128)(2,1)S(1)}, u32[]{:S(2)}, u32[]{:S(2)}) %collective-permute-start.18) | collective-permute-done | bytes 262176 | tf_op jit(solution)/shard_map/ppermute | solution.py:46
  83.3 0.7 collective-permute-start.19
  84.2 0.7 collective-permute-start.20
  85.1 0.7 collective-permute-start.21
  86.2 0.7 collective-permute-start.22
  87.1 0.7 collective-permute-start.23
  87.8 6.7 %collective-permute-start.25 = (bf16[128,512]{1,0:T(8,128)(2,1)S(1)}, bf16[128,512]{1,0:T(8,128)(2,1)S(1)}, u32[]{:S(2)}, u32[]{:S(2)}) collective-permute-start(bf16[128,512]{1,0:T(8,128)(2,1)S(1)} %copy-done.2), channel_id=1, source_target_pairs={{0,32},{1,33},{2,34},{3,35},{4,36},{5,37},{6,38},{7,39},{8,40},{9,... | collective-permute-start | bytes 393224 | tf_op jit(solution)/shard_map/ppermute | solution.py:46
  94.7 0.7 collective-permute-start.24
  95.4 11.8 %collective-permute-done.25 = bf16[128,512]{1,0:T(8,128)(2,1)S(1)} collective-permute-done((bf16[128,512]{1,0:T(8,128)(2,1)S(1)}, bf16[128,512]{1,0:T(8,128)(2,1)S(1)}, u32[]{:S(2)}, u32[]{:S(2)}) %collective-permute-start.25) | collective-permute-done | bytes 131104 | tf_op jit(solution)/shard_map/ppermute | solution.py:46
  108.0 0.7 collective-permute-start.26
  108.9 0.7 collective-permute-start.27
  109.8 0.7 collective-permute-start.28
  110.7 0.7 collective-permute-start.29
  111.9 0.7 collective-permute-start.30
  113.8 1.3 collective-permute-start.32
  115.1 152.5 %collective-permute-done.32.refs_2_ = bf16[2,128,512]{2,1,0:T(8,128)(2,1)S(1)} collective-permute-done((bf16[2,128,512]{2,1,0:T(8,128)(2,1)S(1)}, bf16[2,128,512]{2,1,0:T(8,128)(2,1)S(1)}, u32[]{:S(2)}, u32[]{:S(2)}) %collective-permute-start.32) | collective-permute-done | bytes 262176 | tf_op jit(solution)/shard_map/ppermute | solution.py:46
  267.6 4.2 %layer_curvature.1 = (bf16[256,2048]{1,0:T(8,128)(2,1)S(1)}, f32[256,2048]{1,0:T(8,128)S(1)}) custom-call(s32[1]{0:T(128)} %bitcast.refs_0_, s32[1]{0:T(128)} %bitcast.1.refs_1_, bf16[2,128,512]{2,1,0:T(8,128)(2,1)S(1)} %collective-permute-done.32.refs_2_, bf16[2048,512]{1,0:T(8,128)(2,1)S(1)} %bitcast.48, ...), custom_call_target="tpu_custom_call" | custom-call | tf_op jit(solution)/shard_map/layer_curvature/pallas_call | solution.py:478
  271.7 1.9 collective-permute-start.33
  273.7 2.6 collective-permute-done.33
  276.6 17.3 %all_to_all.10 = bf16[4,64,2048]{2,1,0:T(8,128)(2,1)S(1)} all-to-all(bf16[4,64,2048]{2,1,0:T(8,128)(2,1)S(1)} %bitcast.50), channel_id=1, replica_groups=mesh['zh'=2,'x'=4,'b4'=2,'b2'=2,'b1'=2,'y'=4,'c'=2] {'y'}, dimensions={0} | all-to-all | bytes 2097152 | tf_op jit(solution)/shard_map/all_to_all | solution.py:528
  293.9 0.9 reduce_sum.23
  294.8 11.9 %all-to-all-start.1 = ((bf16[8,8,2048]{2,1,0:T(8,128)(2,1)}), bf16[8,8,2048]{2,1,0:T(8,128)(2,1)S(1)}, u32[]{:S(2)}, u32[]{:S(2)}) async-start(bf16[8,8,2048]{2,1,0:T(8,128)(2,1)} %bitcast.13), calls=%async_computation.1 | async-start | bytes 524288 | tf_op jit(solution)/shard_map/all_to_all | solution.py:530
  306.7 15.5 %all-to-all-done.1 = bf16[8,8,2048]{2,1,0:T(8,128)(2,1)S(1)} async-done(((bf16[8,8,2048]{2,1,0:T(8,128)(2,1)}), bf16[8,8,2048]{2,1,0:T(8,128)(2,1)S(1)}, u32[]{:S(2)}, u32[]{:S(2)}) %all-to-all-start.1) | async-done | bytes 262176 | tf_op jit(solution)/shard_map/all_to_all | solution.py:530
  322.3 1.4 bitcast_multiply_fusion
  (99 shorter events, 8.4 us)
Async XLA Ops:
  0.0 15.4 %copy-start = (bf16[128,512]{1,0:T(8,128)(2,1)S(1)}, bf16[128,512]{1,0:T(8,128)(2,1)}, u32[]{:S(2)}) copy-start(bf16[128,512]{1,0:T(8,128)(2,1)} %param.5) | copy-start | bytes 393220
  0.0 15.8 %collective-permute-start = (bf16[8,2048]{1,0:T(8,128)(2,1)}, bf16[8,2048]{1,0:T(8,128)(2,1)S(1)}, u32[]{:S(2)}, u32[]{:S(2)}) collective-permute-start(bf16[8,2048]{1,0:T(8,128)(2,1)} %bitcast.51), channel_id=1, source_target_pairs={{0,32},{1,33},{2,34},{3,35},{4,36},{5,37},{6,38},{7,39},{8,40},{9,... | collective-permute-start | bytes 98312 | tf_op jit(solution)/shard_map/ppermute | solution.py:46
  10.6 5.2 %copy-start.1 = (bf16[1,8,2048]{2,1,0:T(8,128)(2,1)S(1)}, bf16[1,8,2048]{2,1,0:T(8,128)(2,1)}, u32[]{:S(2)}) copy-start(bf16[1,8,2048]{2,1,0:T(8,128)(2,1)} %param.7) | copy-start | bytes 98308
  10.6 10.4 %collective-permute-start.9 = (bf16[32,512]{1,0:T(8,128)(2,1)S(1)}, bf16[32,512]{1,0:T(8,128)(2,1)S(1)}, u32[]{:S(2)}, u32[]{:S(2)}) collective-permute-start(bf16[32,512]{1,0:T(8,128)(2,1)S(1)} %convolution_bitcast_fusion.2), channel_id=1, source_target_pairs={{0,32},{1,33},{2,34},{3,35},{4,36},{5,37},{6,38},{7,39},{8,40},{9,... | collective-permute-start | bytes 98312 | tf_op jit(solution)/shard_map/ppermute | solution.py:46
  15.8 10.1 %collective-permute-start.1 = (bf16[16,2048]{1,0:T(8,128)(2,1)S(1)}, bf16[16,2048]{1,0:T(8,128)(2,1)S(1)}, u32[]{:S(2)}, u32[]{:S(2)}) collective-permute-start(bf16[16,2048]{1,0:T(8,128)(2,1)S(1)} %pad_maximum_fusion.12), channel_id=1, source_target_pairs={{0,16},{1,17},{2,18},{3,19},{4,20},{5,21},{6,22},{7,23},{8,24},{9,... | collective-permute-start | bytes 196616 | tf_op jit(solution)/shard_map/ppermute | solution.py:46
  21.1 8.4 %collective-permute-start.10 = (bf16[64,512]{1,0:T(8,128)(2,1)S(1)}, bf16[64,512]{1,0:T(8,128)(2,1)S(1)}, u32[]{:S(2)}, u32[]{:S(2)}) collective-permute-start(bf16[64,512]{1,0:T(8,128)(2,1)S(1)} %pad_maximum_fusion.13), channel_id=1, source_target_pairs={{0,16},{1,17},{2,18},{3,19},{4,20},{5,21},{6,22},{7,23},{8,24},{9,... | collective-permute-start | bytes 196616 | tf_op jit(solution)/shard_map/ppermute | solution.py:46
  26.0 7.9 %collective-permute-start.2 = (bf16[32,2048]{1,0:T(8,128)(2,1)S(1)}, bf16[32,2048]{1,0:T(8,128)(2,1)S(1)}, u32[]{:S(2)}, u32[]{:S(2)}) collective-permute-start(bf16[32,2048]{1,0:T(8,128)(2,1)S(1)} %pad_maximum_fusion.10), channel_id=1, source_target_pairs={{0,8},{1,9},{2,10},{3,11},{4,12},{5,13},{6,14},{7,15},{8,0},{9,1},... | collective-permute-start | bytes 393224 | tf_op jit(solution)/shard_map/ppermute | solution.py:46
  29.5 11.2 %collective-permute-start.11 = (bf16[128,512]{1,0:T(8,128)(2,1)S(1)}, bf16[128,512]{1,0:T(8,128)(2,1)S(1)}, u32[]{:S(2)}, u32[]{:S(2)}) collective-permute-start(bf16[128,512]{1,0:T(8,128)(2,1)S(1)} %pad_maximum_fusion.11), channel_id=1, source_target_pairs={{0,8},{1,9},{2,10},{3,11},{4,12},{5,13},{6,14},{7,15},{8,0},{9,1},... | collective-permute-start | bytes 393224 | tf_op jit(solution)/shard_map/ppermute | solution.py:46
  34.0 12.4 %collective-permute-start.3 = (bf16[64,1024]{1,0:T(8,128)(2,1)S(1)}, bf16[64,1024]{1,0:T(8,128)(2,1)S(1)}, u32[]{:S(2)}, u32[]{:S(2)}) collective-permute-start(bf16[64,1024]{1,0:T(8,128)(2,1)S(1)} %get-tuple-element.133), channel_id=1, source_target_pairs={{0,2},{1,3},{2,0},{3,1},{4,6},{5,7},{6,4},{7,5},{8,10},{9,11},{10,... | collective-permute-start | bytes 393224 | tf_op jit(solution)/shard_map/ppermute | solution.py:46
  37.1 12.9 %collective-permute-start.6 = (bf16[64,1024]{1,0:T(8,128)(2,1)S(1)}, bf16[64,1024]{1,0:T(8,128)(2,1)S(1)}, u32[]{:S(2)}, u32[]{:S(2)}) collective-permute-start(bf16[64,1024]{1,0:T(8,128)(2,1)S(1)} %get-tuple-element.134), channel_id=1, source_target_pairs={{0,6},{1,7},{2,4},{3,5},{4,2},{5,3},{6,0},{7,1},{8,14},{9,15},{10,... | collective-permute-start | bytes 393224 | tf_op jit(solution)/shard_map/ppermute | solution.py:46
  40.8 13.1 %collective-permute-start.12 = (bf16[256,256]{1,0:T(8,128)(2,1)S(1)}, bf16[256,256]{1,0:T(8,128)(2,1)S(1)}, u32[]{:S(2)}, u32[]{:S(2)}) collective-permute-start(bf16[256,256]{1,0:T(8,128)(2,1)S(1)} %get-tuple-element.123), channel_id=1, source_target_pairs={{0,2},{1,3},{2,0},{3,1},{4,6},{5,7},{6,4},{7,5},{8,10},{9,11},{10,... | collective-permute-start | bytes 393224 | tf_op jit(solution)/shard_map/ppermute | solution.py:46
  44.0 12.1 %collective-permute-start.15 = (bf16[256,256]{1,0:T(8,128)(2,1)S(1)}, bf16[256,256]{1,0:T(8,128)(2,1)S(1)}, u32[]{:S(2)}, u32[]{:S(2)}) collective-permute-start(bf16[256,256]{1,0:T(8,128)(2,1)S(1)} %get-tuple-element.124), channel_id=1, source_target_pairs={{0,6},{1,7},{2,4},{3,5},{4,2},{5,3},{6,0},{7,1},{8,14},{9,15},{10,... | collective-permute-start | bytes 393224 | tf_op jit(solution)/shard_map/ppermute | solution.py:46
  46.5 12.5 %collective-permute-start.4 = (bf16[128,1024]{1,0:T(8,128)(2,1)S(1)}, bf16[128,1024]{1,0:T(8,128)(2,1)S(1)}, u32[]{:S(2)}, u32[]{:S(2)}) collective-permute-start(bf16[128,1024]{1,0:T(8,128)(2,1)S(1)} %pad_maximum_fusion.4), channel_id=1, source_target_pairs={{0,6},{1,7},{2,4},{3,5},{4,2},{5,3},{6,0},{7,1},{8,14},{9,15},{10,... | collective-permute-start | bytes 786440 | tf_op jit(solution)/shard_map/ppermute | solution.py:46
  50.0 16.7 %collective-permute-start.7 = (bf16[128,1024]{1,0:T(8,128)(2,1)S(1)}, bf16[128,1024]{1,0:T(8,128)(2,1)S(1)}, u32[]{:S(2)}, u32[]{:S(2)}) collective-permute-start(bf16[128,1024]{1,0:T(8,128)(2,1)S(1)} %pad_maximum_fusion.5), channel_id=1, source_target_pairs={{0,2},{1,3},{2,0},{3,1},{4,6},{5,7},{6,4},{7,5},{8,10},{9,11},{10,... | collective-permute-start | bytes 786440 | tf_op jit(solution)/shard_map/ppermute | solution.py:46
  53.9 8.3 %collective-permute-start.13 = (bf16[512,256]{1,0:T(8,128)(2,1)S(1)}, bf16[512,256]{1,0:T(8,128)(2,1)S(1)}, u32[]{:S(2)}, u32[]{:S(2)}) collective-permute-start(bf16[512,256]{1,0:T(8,128)(2,1)S(1)} %pad_maximum_fusion.6), channel_id=1, source_target_pairs={{0,6},{1,7},{2,4},{3,5},{4,2},{5,3},{6,0},{7,1},{8,14},{9,15},{10,... | collective-permute-start | bytes 786440 | tf_op jit(solution)/shard_map/ppermute | solution.py:46
  56.2 8.3 %collective-permute-start.16 = (bf16[512,256]{1,0:T(8,128)(2,1)S(1)}, bf16[512,256]{1,0:T(8,128)(2,1)S(1)}, u32[]{:S(2)}, u32[]{:S(2)}) collective-permute-start(bf16[512,256]{1,0:T(8,128)(2,1)S(1)} %pad_maximum_fusion.7), channel_id=1, source_target_pairs={{0,2},{1,3},{2,0},{3,1},{4,6},{5,7},{6,4},{7,5},{8,10},{9,11},{10,... | collective-permute-start | bytes 786440 | tf_op jit(solution)/shard_map/ppermute | solution.py:46
  59.2 10.8 %collective-permute-start.5 = (bf16[256,1024]{1,0:T(8,128)(2,1)S(1)}, bf16[256,1024]{1,0:T(8,128)(2,1)S(1)}, u32[]{:S(2)}, u32[]{:S(2)}) collective-permute-start(bf16[256,1024]{1,0:T(8,128)(2,1)S(1)} %pad_maximum_fusion), channel_id=1, source_target_pairs={{0,1},{1,0},{2,3},{3,2},{4,5},{5,4},{6,7},{7,6},{8,9},{9,8},{10,11... | collective-permute-start | bytes 1572872 | tf_op jit(solution)/shard_map/ppermute | solution.py:46
  62.3 6.7 %collective-permute-start.14 = (bf16[1024,256]{1,0:T(8,128)(2,1)S(1)}, bf16[1024,256]{1,0:T(8,128)(2,1)S(1)}, u32[]{:S(2)}, u32[]{:S(2)}) collective-permute-start(bf16[1024,256]{1,0:T(8,128)(2,1)S(1)} %pad_maximum_fusion.2), channel_id=1, source_target_pairs={{0,1},{1,0},{2,3},{3,2},{4,5},{5,4},{6,7},{7,6},{8,9},{9,8},{10,11... | collective-permute-start | bytes 1572872 | tf_op jit(solution)/shard_map/ppermute | solution.py:46
  64.6 4.7 %collective-permute-start.17 = (bf16[1024,256]{1,0:T(8,128)(2,1)S(1)}, bf16[1024,256]{1,0:T(8,128)(2,1)S(1)}, u32[]{:S(2)}, u32[]{:S(2)}) collective-permute-start(bf16[1024,256]{1,0:T(8,128)(2,1)S(1)} %pad_maximum_fusion.3), channel_id=1, source_target_pairs={{0,1},{1,0},{2,3},{3,2},{4,5},{5,4},{6,7},{7,6},{8,9},{9,8},{10,11... | collective-permute-start | bytes 1572872 | tf_op jit(solution)/shard_map/ppermute | solution.py:46
  66.9 3.8 %collective-permute-start.8 = (bf16[256,1024]{1,0:T(8,128)(2,1)S(1)}, bf16[256,1024]{1,0:T(8,128)(2,1)S(1)}, u32[]{:S(2)}, u32[]{:S(2)}) collective-permute-start(bf16[256,1024]{1,0:T(8,128)(2,1)S(1)} %pad_maximum_fusion.1), channel_id=1, source_target_pairs={{0,1},{1,0},{2,3},{3,2},{4,5},{5,4},{6,7},{7,6},{8,9},{9,8},{10,11... | collective-permute-start | bytes 1572872 | tf_op jit(solution)/shard_map/ppermute | solution.py:46
  75.6 7.5 %collective-permute-start.18 = (bf16[2,128,512]{2,1,0:T(8,128)(2,1)S(1)}, bf16[2,128,512]{2,1,0:T(8,128)(2,1)S(1)}, u32[]{:S(2)}, u32[]{:S(2)}) collective-permute-start(bf16[2,128,512]{2,1,0:T(8,128)(2,1)S(1)} %get-tuple-element.53), channel_id=1, source_target_pairs={{0,64},{1,65},{2,66},{3,67},{4,68},{5,69},{6,70},{7,71},{8,72},{9,... | collective-permute-start | bytes 786440 | tf_op jit(solution)/shard_map/ppermute | solution.py:46
  83.3 0.7 collective-permute-start.19
  84.2 0.7 collective-permute-start.20
  85.1 0.7 collective-permute-start.21
  86.2 0.7 collective-permute-start.22
  86.9 0.9 copy-start.2
  87.1 7.4 %collective-permute-start.23 = (bf16[2,128,512]{2,1,0:T(8,128)(2,1)S(1)}, bf16[2,128,512]{2,1,0:T(8,128)(2,1)S(1)}, u32[]{:S(2)}, u32[]{:S(2)}) collective-permute-start(bf16[2,128,512]{2,1,0:T(8,128)(2,1)S(1)} %get-tuple-element.73), channel_id=1, source_target_pairs={{320,384},{321,385},{322,386},{323,387},{324,388},{325,389},{326,3... | collective-permute-start | bytes 786440 | tf_op jit(solution)/shard_map/ppermute | solution.py:46
  87.8 19.4 %collective-permute-start.25 = (bf16[128,512]{1,0:T(8,128)(2,1)S(1)}, bf16[128,512]{1,0:T(8,128)(2,1)S(1)}, u32[]{:S(2)}, u32[]{:S(2)}) collective-permute-start(bf16[128,512]{1,0:T(8,128)(2,1)S(1)} %copy-done.2), channel_id=1, source_target_pairs={{0,32},{1,33},{2,34},{3,35},{4,36},{5,37},{6,38},{7,39},{8,40},{9,... | collective-permute-start | bytes 393224 | tf_op jit(solution)/shard_map/ppermute | solution.py:46
  94.7 12.8 %collective-permute-start.24 = (bf16[2,128,512]{2,1,0:T(8,128)(2,1)S(1)}, bf16[2,128,512]{2,1,0:T(8,128)(2,1)S(1)}, u32[]{:S(2)}, u32[]{:S(2)}) collective-permute-start(bf16[2,128,512]{2,1,0:T(8,128)(2,1)S(1)} %get-tuple-element.77), channel_id=1, source_target_pairs={{384,448},{385,449},{386,450},{387,451},{388,452},{389,453},{390,4... | collective-permute-start | bytes 786440 | tf_op jit(solution)/shard_map/ppermute | solution.py:46
  108.0 0.7 collective-permute-start.26
  108.9 0.7 collective-permute-start.27
  109.8 0.7 collective-permute-start.28
  110.7 0.7 collective-permute-start.29
  111.9 0.7 collective-permute-start.30
  112.8 0.7 collective-permute-start.31
  113.8 153.8 %collective-permute-start.32 = (bf16[2,128,512]{2,1,0:T(8,128)(2,1)S(1)}, bf16[2,128,512]{2,1,0:T(8,128)(2,1)S(1)}, u32[]{:S(2)}, u32[]{:S(2)}) collective-permute-start(bf16[2,128,512]{2,1,0:T(8,128)(2,1)S(1)} %get-tuple-element.97), channel_id=1, source_target_pairs={{64,0},{65,1},{66,2},{67,3},{68,4},{69,5},{70,6},{71,7},{72,8},{73... | collective-permute-start | bytes 786440 | tf_op jit(solution)/shard_map/ppermute | solution.py:46
  271.7 4.6 %collective-permute-start.33 = (bf16[256,2048]{1,0:T(8,128)(2,1)S(1)}, bf16[256,2048]{1,0:T(8,128)(2,1)S(1)}, u32[]{:S(2)}, u32[]{:S(2)}) collective-permute-start(bf16[256,2048]{1,0:T(8,128)(2,1)S(1)} %get-tuple-element.100), channel_id=1, source_target_pairs={{0,1},{1,0},{2,3},{3,2},{4,5},{5,4},{6,7},{7,6},{8,9},{9,8},{10,11... | collective-permute-start | bytes 3145736 | tf_op jit(solution)/shard_map/ppermute | solution.py:46
  294.8 27.5 %all-to-all-start.1 = ((bf16[8,8,2048]{2,1,0:T(8,128)(2,1)}), bf16[8,8,2048]{2,1,0:T(8,128)(2,1)S(1)}, u32[]{:S(2)}, u32[]{:S(2)}) async-start(bf16[8,8,2048]{2,1,0:T(8,128)(2,1)} %bitcast.13), calls=%async_computation.1 | async-start | bytes 524288 | tf_op jit(solution)/shard_map/all_to_all | solution.py:530

commit v2 on v1

v2 whole, which is shorter than its diff:
```python
import functools
import itertools

import jax
import jax.numpy as jnp
from jax import lax
from jax.experimental import pallas as pl
from jax.experimental.pallas import tpu as pltpu
from jax.sharding import Mesh, PartitionSpec as P

EPSILON = 1e-05
SQRT_HALF = 0.7071067811865476
INV_ROOT_TWO_PI = 0.3989422804014327
CONTRACT_LAST = (((1,), (1,)), ((), ()))
CONTRACT_FIRST = (((0,), (0,)), ((), ()))

NAMES = ("zh", "x", "b4", "b2", "b1", "y", "c")
SIZES = (2, 4, 2, 2, 2, 4, 2)
SECTION = ("zh", "x")
DP = ("b4", "b2", "b1", "y", "c")
LAYERS = 8
FEATURES = 512
HIDDEN = 2048
MICRO = 2
ROWS = 64
UNROLL = 2
TOKENS = 8192
CHUNK = 512
CHUNKS = HIDDEN // CHUNK
VMEM_BYTES = 8 * 1024 * 1024
WHOLE = pl.BlockSpec(memory_space=pltpu.VMEM)
SMEM = pl.BlockSpec(memory_space=pltpu.SMEM)


def flat(place):
    index = 0
    for size, at in zip(SIZES, place):
        index = index * size + at
    return index


def routed(value, route):
    pairs = []
    for place in itertools.product(*(range(size) for size in SIZES)):
        there = route(*place)
        if there is not None:
            pairs.append((flat(place), flat(there)))
    return lax.ppermute(value, NAMES, pairs)


def swap_b4(zh, x, b4, b2, b1, y, c):
    return (zh, x, 1 - b4, b2, b1, y, c)


def swap_b2(zh, x, b4, b2, b1, y, c):
    return (zh, x, b4, 1 - b2, b1, y, c)


def swap_b1(zh, x, b4, b2, b1, y, c):
    return (zh, x, b4, b2, 1 - b1, y, c)


def swap_even(zh, x, b4, b2, b1, y, c):
    return (zh, x, b4, b2, b1, y ^ 1, c)


def swap_odd(zh, x, b4, b2, b1, y, c):
    return (zh, x, b4, b2, b1, y ^ 3, c)


def swap_core(zh, x, b4, b2, b1, y, c):
    return (zh, x, b4, b2, b1, y, 1 - c)


def up_from(section):
    def route(zh, x, b4, b2, b1, y, c):
        if zh * 4 + x != section:
            return None
        if x == 3:
            return (zh + 1, 0, 1 - b4, b2, b1, y, c)
        return (zh, x + 1, b4, b2, b1, y, c)

    return route


def down_from(section):
    def route(zh, x, b4, b2, b1, y, c):
        if zh * 4 + x != section:
            return None
        if x == 0:
            return (zh - 1, 3, 1 - b4, b2, b1, y, c)
        return (zh, x - 1, b4, b2, b1, y, c)

    return route


def merged(own, other, bit):
    first = bit == 0
    return jnp.concatenate([jnp.where(first, own, other), jnp.where(first, other, own)], axis=0)


def gathered(block):
    block = merged(block, routed(block, swap_b4), lax.axis_index("b4"))
    block = merged(block, routed(block, swap_b2), lax.axis_index("b2"))
    block = merged(block, routed(block, swap_b1), lax.axis_index("b1"))
    rows, half = block.shape[0], block.shape[1] // 2
    y = lax.axis_index("y")
    left, right = block[:, :half], block[:, half:]
    left_two = merged(left, routed(left, swap_even), y % 2)
    right_two = merged(right, routed(right, swap_odd), y // 2)
    left_four = merged(left_two, routed(left_two, swap_odd), y // 2)
    other = routed(right_two, swap_even)
    outer = (y == 0) | (y == 3)
    own_a, own_b, oth_a, oth_b = right_two[:rows], right_two[rows:], other[:rows], other[rows:]
    right_four = jnp.concatenate(
        [
            jnp.where(outer, own_a, oth_a),
            jnp.where(outer, oth_a, own_a),
            jnp.where(outer, oth_b, own_b),
            jnp.where(outer, own_b, oth_b),
        ],
        axis=0,
    )
    core = lax.axis_index("c")
    return jnp.concatenate(
        [
            merged(left_four, routed(left_four, swap_core), core),
            merged(right_four, routed(right_four, swap_core), core),
        ],
        axis=1,
    )


def feature_order():
    position = lax.broadcasted_iota(jnp.int32, (FEATURES, FEATURES), 1)
    natural = lax.broadcasted_iota(jnp.int32, (FEATURES, FEATURES), 0)
    core, y = position // 256, (position // 64) % 4
    b1, b2, b4, row = (position // 32) % 2, (position // 16) % 2, (position // 8) % 2, position % 8
    return (natural == (b4 * 4 + b2 * 2 + b1) * 64 + y * 16 + core * 8 + row).astype(jnp.bfloat16)


def row_mean(values):
    return jnp.mean(values, axis=-1, keepdims=True)


def columns(chunk):
    return pl.ds(pl.multiple_of(chunk * CHUNK, CHUNK), CHUNK)


def forward_kernel(tick, *refs):
    last = tick == LAYERS - 1
    section, pair, w_in, probe, w_out = refs[:5]
    refs = refs[5:]
    if last:
        goal, refs = refs[0], refs[1:]
    pair_out, norm, stat, slope_out, lhs, acc = refs

    @pl.when(section[0] == tick)
    def _():
        inflow = pair[0].astype(jnp.float32)
        inflow_t = pair[1].astype(jnp.float32)
        centred = inflow - row_mean(inflow)
        rscale = lax.rsqrt(row_mean(centred * centred) + EPSILON)
        normed = centred * rscale
        tangent_dot = row_mean(normed * inflow_t)
        normed_t = rscale * (inflow_t - row_mean(inflow_t) - normed * tangent_dot)
        norm[0] = normed
        norm[1] = normed_t
        stat[0] = jnp.broadcast_to(rscale, (ROWS, 128))
        stat[1] = jnp.broadcast_to(tangent_dot, (ROWS, 128))
        lhs[:ROWS] = normed.astype(jnp.bfloat16)
        lhs[ROWS:] = normed_t.astype(jnp.bfloat16)
        acc[:ROWS] = inflow
        acc[ROWS:] = inflow_t

        def step(chunk, carry):
            both = jnp.dot(lhs[...], w_in[:, columns(chunk)], preferred_element_type=jnp.float32)
            preact = both[:ROWS]
            preact_t = both[ROWS:] + jnp.dot(lhs[:ROWS], probe[:, columns(chunk)], preferred_element_type=jnp.float32)
            normal_cdf = 0.5 * (1.0 + lax.erf(preact * SQRT_HALF))
            density = INV_ROOT_TWO_PI * jnp.exp(-0.5 * preact * preact)
            slope = normal_cdf + preact * density
            slope_out[0, :, columns(chunk)] = slope
            slope_out[1, :, columns(chunk)] = density * (2.0 - preact * preact) * preact_t
            hidden = jnp.concatenate([preact * normal_cdf, slope * preact_t], axis=0).astype(jnp.bfloat16)
            acc[...] += jnp.dot(hidden, w_out[columns(chunk), :], preferred_element_type=jnp.float32)
            return carry

        lax.fori_loop(0, CHUNKS, step, 0, unroll=UNROLL)
        if last:
            pair_out[0] = ((acc[:ROWS] - goal[...].astype(jnp.float32)) / TOKENS).astype(jnp.bfloat16)
            pair_out[1] = (acc[ROWS:] / TOKENS).astype(jnp.bfloat16)
        else:
            pair_out[0] = acc[:ROWS].astype(jnp.bfloat16)
            pair_out[1] = acc[ROWS:].astype(jnp.bfloat16)


NORM = jax.ShapeDtypeStruct((2, ROWS, FEATURES), jnp.float32)
STAT = jax.ShapeDtypeStruct((2, ROWS, 128), jnp.float32)
SLOPE = jax.ShapeDtypeStruct((2, ROWS, HIDDEN), jnp.float32)
PAIR = jax.ShapeDtypeStruct((2, ROWS, FEATURES), jnp.bfloat16)
GRADS = jax.ShapeDtypeStruct((2 * ROWS, HIDDEN), jnp.bfloat16)
PARAMS = pltpu.CompilerParams(vmem_limit_bytes=VMEM_BYTES)


def forward_call(tick, section, pair, w_in, probe, w_out, goal):
    last = tick == LAYERS - 1
    operands = [section, pair, w_in, probe, w_out] + ([goal] if last else [])
    return pl.pallas_call(
        functools.partial(forward_kernel, tick),
        out_shape=[PAIR, NORM, STAT, SLOPE],
        in_specs=[SMEM] + [WHOLE] * (len(operands) - 1),
        out_specs=[WHOLE] * 4,
        scratch_shapes=[
            pltpu.VMEM((2 * ROWS, FEATURES), jnp.bfloat16),
            pltpu.VMEM((2 * ROWS, FEATURES), jnp.float32),
        ],
        compiler_params=PARAMS,
        name=f"layer_up_{tick}",
    )(*operands)


def hidden_grads(pair, w_out, slope, chunk):
    both = lax.dot_general(
        pair[...].reshape(2 * ROWS, FEATURES),
        w_out[columns(chunk), :],
        CONTRACT_LAST,
        preferred_element_type=jnp.float32,
    )
    grad_hidden, grad_hidden_t = both[:ROWS], both[ROWS:]
    slope_chunk = slope[0, :, columns(chunk)]
    grad_pre = grad_hidden * slope_chunk
    grad_pre_t = grad_hidden_t * slope_chunk + grad_hidden * slope[1, :, columns(chunk)]
    return grad_pre.astype(jnp.bfloat16), grad_pre_t.astype(jnp.bfloat16)


def norm_apply(values, normed, rscale):
    return rscale * (values - row_mean(values) - normed * row_mean(normed * values))


def backward_kernel(tick, *refs):
    section, pair, w_in, probe, w_out, norm, stat, slope = refs[:8]
    pair_out, grads, acc, acc_t = refs[8:]

    @pl.when(section[0] == LAYERS - 1 - tick)
    def _():
        acc[...] = jnp.zeros_like(acc)
        acc_t[...] = jnp.zeros_like(acc_t)

        def step(chunk, carry):
            low_grad, low_grad_t = hidden_grads(pair, w_out, slope, chunk)
            both = jnp.concatenate([low_grad_t, low_grad], axis=0)
            grads[:, columns(chunk)] = both
            acc[...] += lax.dot_general(
                both, w_in[:, columns(chunk)], CONTRACT_LAST, preferred_element_type=jnp.float32
            )
            acc_t[...] += lax.dot_general(
                low_grad, probe[:, columns(chunk)], CONTRACT_LAST, preferred_element_type=jnp.float32
            )
            return carry

        lax.fori_loop(0, CHUNKS, step, 0, unroll=UNROLL)
        normed, normed_t = norm[0], norm[1]
        rscale, tangent_dot = stat[0][:, :1], stat[1][:, :1]
        grad_norm = acc[ROWS:]
        grad_norm_t = acc[:ROWS] + acc_t[...]
        through = norm_apply(grad_norm, normed, rscale)
        through_t = (
            norm_apply(grad_norm_t, normed, rscale)
            - rscale * tangent_dot * through
            - rscale * (normed_t * row_mean(normed * grad_norm) + normed * row_mean(normed_t * grad_norm))
        )
        pair_out[0] = (pair[0].astype(jnp.float32) + through).astype(jnp.bfloat16)
        pair_out[1] = (pair[1].astype(jnp.float32) + through_t).astype(jnp.bfloat16)


def backward_call(tick, section, pair, w_in, probe, w_out, kept):
    operands = [section, pair, w_in, probe, w_out, *kept]
    return pl.pallas_call(
        functools.partial(backward_kernel, tick),
        out_shape=[PAIR, GRADS],
        in_specs=[SMEM] + [WHOLE] * (len(operands) - 1),
        out_specs=[WHOLE] * 2,
        scratch_shapes=[
            pltpu.VMEM((2 * ROWS, FEATURES), jnp.float32),
            pltpu.VMEM((ROWS, FEATURES), jnp.float32),
        ],
        compiler_params=PARAMS,
        name=f"layer_down_{tick}",
    )(*operands)


def core_half(index):
    return pl.ds(pl.multiple_of(index * (FEATURES // 2), FEATURES // 2), FEATURES // 2)


def curvature_kernel(final, *refs):
    section, core, pair, w_out, slope = refs[:5]
    norms, refs = refs[5 : 5 + LAYERS], refs[5 + LAYERS :]
    grads, refs = refs[: LAYERS - 1], refs[LAYERS - 1 :]
    if final:
        away_in, stay_in, refs = refs[0], refs[1], refs[2:]
    away, stay, lhs, rhs = refs
    for layer in range(LAYERS):

        @pl.when(section[0] == layer)
        def _():
            lhs[...] = norms[layer][...].reshape(2 * ROWS, FEATURES).astype(jnp.bfloat16)
            if layer:
                rhs[...] = grads[LAYERS - 1 - layer][...]
            else:

                def bottom(chunk, carry):
                    low_grad, low_grad_t = hidden_grads(pair, w_out, slope, chunk)
                    rhs[:, columns(chunk)] = jnp.concatenate([low_grad_t, low_grad], axis=0)
                    return carry

                lax.fori_loop(0, CHUNKS, bottom, 0, unroll=UNROLL)

    def step(chunk, carry):
        now = columns(chunk)

        def product(half):
            return lax.dot_general(lhs[:, core_half(half)], rhs[:, now], CONTRACT_FIRST, preferred_element_type=jnp.float32)

        if final:
            away[:, now] = (away_in[:, now] + product(1 - core[0])).astype(jnp.bfloat16)
            stay[:, now] = stay_in[:, now] + product(core[0])
        else:
            away[:, now] = product(1 - core[0])
            stay[:, now] = product(core[0])
        return carry

    lax.fori_loop(0, CHUNKS, step, 0)


def curvature_call(section, core, pair, w_out, slope, norms, grads, sums):
    half = (FEATURES // 2, HIDDEN)
    final = bool(sums)
    operands = [section, core, pair, w_out, slope, *norms, *grads, *sums]
    return pl.pallas_call(
        functools.partial(curvature_kernel, final),
        out_shape=[
            jax.ShapeDtypeStruct(half, jnp.bfloat16 if final else jnp.float32),
            jax.ShapeDtypeStruct(half, jnp.float32),
        ],
        in_specs=[SMEM, SMEM] + [WHOLE] * (len(operands) - 2),
        out_specs=[WHOLE] * 2,
        scratch_shapes=[
            pltpu.VMEM((2 * ROWS, FEATURES), jnp.bfloat16),
            pltpu.VMEM((2 * ROWS, HIDDEN), jnp.bfloat16),
        ],
        compiler_params=PARAMS,
        name="curvature_last" if final else "curvature_first",
    )(*operands)


def shards(inputs, targets, w_in, w_out, probes):
    section = jnp.reshape(lax.axis_index(SECTION), (1,)).astype(jnp.int32)
    core = jnp.reshape(lax.axis_index("c"), (1,)).astype(jnp.int32)
    order = feature_order()
    full_in = gathered(w_in[0])
    full_out = gathered(jnp.dot(w_out[0], order))
    full_out = (
        full_out.reshape(2, 4, 2, 2, 2, 32, FEATURES).transpose(4, 3, 2, 1, 0, 5, 6).reshape(HIDDEN, FEATURES)
    )
    probe = lax.dot_general(order, probes[0], CONTRACT_FIRST, preferred_element_type=jnp.bfloat16)
    fresh = jnp.dot(inputs, order)
    goal = jnp.dot(routed(targets, swap_b4), order)
    pairs, goals, kept, grads = [], [], [], []
    for micro in range(MICRO):
        rows = slice(micro * ROWS, (micro + 1) * ROWS)
        pairs.append(jnp.stack([fresh[rows], jnp.zeros_like(fresh[rows])]))
        goals.append(goal[rows])
        kept.append([])
        grads.append([])
    for tick in range(LAYERS):
        for micro in range(MICRO):
            pairs[micro], *stores = forward_call(
                tick, section, pairs[micro], full_in, probe, full_out, goals[micro]
            )
            kept[micro].append(stores)
            if tick < LAYERS - 1:
                pairs[micro] = routed(pairs[micro], up_from(tick))
    for tick in range(LAYERS - 1):
        for micro in range(MICRO):
            pairs[micro], low_grads = backward_call(
                tick, section, pairs[micro], full_in, probe, full_out, kept[micro][LAYERS - 1 - tick]
            )
            grads[micro].append(low_grads)
            pairs[micro] = routed(pairs[micro], down_from(LAYERS - 1 - tick))
    sums = ()
    for micro in range(MICRO):
        norms = [stores[0] for stores in kept[micro]]
        sums = curvature_call(
            section, core, pairs[micro], full_out, kept[micro][0][2], norms, grads[micro], sums
        )
    away, stay = sums
    summed = (stay + routed(away, swap_core).astype(jnp.float32)).astype(jnp.bfloat16)
    summed = lax.all_to_all(summed.reshape(4, 64, HIDDEN), "y", 0, 0, tiled=True)
    summed = jnp.sum(summed.astype(jnp.float32), axis=0).astype(jnp.bfloat16)
    summed = lax.all_to_all(summed.reshape(8, 8, HIDDEN), ("b1", "b2", "b4"), 0, 0, tiled=True)
    summed = jnp.sum(summed.astype(jnp.float32), axis=0)
    probe_own = lax.dynamic_slice_in_dim(probes[0], lax.axis_index(DP) * 8, 8, 0)
    return (probe_own.astype(jnp.float32) * summed)[None]


def solution(mesh):
    fine = Mesh(mesh.devices.reshape(SIZES), NAMES)
    return jax.shard_map(
        shards,
        mesh=fine,
        in_specs=(
            P(DP, None),
            P(DP, None),
            P(SECTION, DP, None),
            P(SECTION, DP, None),
            P(SECTION, None, None),
        ),
        out_specs=P(SECTION, DP, None),
        check_vma=False,
    )
```

time: 325 us -> 403 us (1.24)
  starting transfers between devices: 91.5 us -> 239 us
  waiting for transfers between devices: 192 us -> 123 us
    ppermute x34 -> x48, starting transfers between devices: 79.6 us -> 231 us  [routed(): return lax.ppermute(value, NAMES, pairs)]
    ppermute x34 -> x48, waiting for transfers between devices: 176 us -> 107 us  [routed(): return lax.ppermute(value, NAMES, pairs)]
  transfers between devices with their start and end apart: 35 -> 49, of which waited for: 9 -> 8; matrix products, arithmetic and copies ran while one was open for 2% -> 2% of each run, Pallas kernels for 0% -> 1%
where the time goes in v2:
time: 403 us; the launch traced here: 402 us
  starting transfers between devices  239 us (59%)
  waiting for transfers between devices  123 us (31%)
  blocking collectives  18.7 us (5%)
  Pallas kernels  10.4 us (3%)
  other arithmetic  5.03 us (1%)
  matrix products  4.45 us (1%)
    ppermute x48, starting transfers between devices, routed(): return lax.ppermute(value, NAMES, pairs)  231 us
    ppermute x48, waiting for transfers between devices, routed(): return lax.ppermute(value, NAMES, pairs)  107 us
    all_to_all x1, blocking collectives, shards(): lax.all_to_all(summed.reshape(4, 64, HIDDEN), 'y', 0, 0, tiled=True)  18.7 us
    all_to_all x1, waiting for transfers between devices, shards(): lax.all_to_all(summed.reshape(8, 8, HIDDEN), ('b1', 'b2', 'b4'), 0, 0, ti...  15.5 us
    all_to_all x1, starting transfers between devices, shards(): lax.all_to_all(summed.reshape(8, 8, HIDDEN), ('b1', 'b2', 'b4'), 0, 0, ti...  8.27 us
  transfers between devices with their start and end apart: 49, of which 8 were waited for; matrix products, arithmetic and copies ran while one was open for 2% of the time, Pallas kernels for 1%

profile of v2, /device:TPU:8, one launch (start us, length us, event | category | flops | bytes accessed | tf_op | source)
XLA Modules:
  0.0 402.0 jit_solution(4401471080543987106)
XLA Ops:
  0.0 9.2 %collective-permute-start = (bf16[8,2048]{1,0:T(8,128)(2,1)}, bf16[8,2048]{1,0:T(8,128)(2,1)S(1)}, u32[]{:S(2)}, u32[]{:S(2)}) collective-permute-start(bf16[8,2048]{1,0:T(8,128)(2,1)} %bitcast.69), channel_id=1, source_target_pairs={{0,32},{1,33},{2,34},{3,35},{4,36},{5,37},{6,38},{7,39},{8,40},{9,... | collective-permute-start | bytes 98312 | tf_op jit(solution)/shard_map/ppermute | solution.py:48
  9.6 1.0 convolution_bitcast_fusion.2
  10.6 15.8 %collective-permute-start.9 = (bf16[32,512]{1,0:T(8,128)(2,1)S(1)}, bf16[32,512]{1,0:T(8,128)(2,1)S(1)}, u32[]{:S(2)}, u32[]{:S(2)}) collective-permute-start(bf16[32,512]{1,0:T(8,128)(2,1)S(1)} %convolution_bitcast_fusion.2), channel_id=1, source_target_pairs={{0,32},{1,33},{2,34},{3,35},{4,36},{5,37},{6,38},{7,39},{8,40},{9,... | collective-permute-start | bytes 98312 | tf_op jit(solution)/shard_map/ppermute | solution.py:48
  26.7 2.9 fusion.refs_3_
  29.8 19.0 %collective-permute-start.1 = (bf16[16,2048]{1,0:T(8,128)(2,1)S(1)}, bf16[16,2048]{1,0:T(8,128)(2,1)S(1)}, u32[]{:S(2)}, u32[]{:S(2)}) collective-permute-start(bf16[16,2048]{1,0:T(8,128)(2,1)S(1)} %pad_maximum_fusion.12), channel_id=1, source_target_pairs={{0,16},{1,17},{2,18},{3,19},{4,20},{5,21},{6,22},{7,23},{8,24},{9,... | collective-permute-start | bytes 196616 | tf_op jit(solution)/shard_map/ppermute | solution.py:48
  48.8 19.0 %collective-permute-start.10 = (bf16[64,512]{1,0:T(8,128)(2,1)S(1)}, bf16[64,512]{1,0:T(8,128)(2,1)S(1)}, u32[]{:S(2)}, u32[]{:S(2)}) collective-permute-start(bf16[64,512]{1,0:T(8,128)(2,1)S(1)} %pad_maximum_fusion.13), channel_id=1, source_target_pairs={{0,16},{1,17},{2,18},{3,19},{4,20},{5,21},{6,22},{7,23},{8,24},{9,... | collective-permute-start | bytes 196616 | tf_op jit(solution)/shard_map/ppermute | solution.py:48
  67.9 19.0 %collective-permute-start.2 = (bf16[32,2048]{1,0:T(8,128)(2,1)S(1)}, bf16[32,2048]{1,0:T(8,128)(2,1)S(1)}, u32[]{:S(2)}, u32[]{:S(2)}) collective-permute-start(bf16[32,2048]{1,0:T(8,128)(2,1)S(1)} %pad_maximum_fusion.10), channel_id=1, source_target_pairs={{0,8},{1,9},{2,10},{3,11},{4,12},{5,13},{6,14},{7,15},{8,0},{9,1},... | collective-permute-start | bytes 393224 | tf_op jit(solution)/shard_map/ppermute | solution.py:48
  87.0 19.0 %collective-permute-start.11 = (bf16[128,512]{1,0:T(8,128)(2,1)S(1)}, bf16[128,512]{1,0:T(8,128)(2,1)S(1)}, u32[]{:S(2)}, u32[]{:S(2)}) collective-permute-start(bf16[128,512]{1,0:T(8,128)(2,1)S(1)} %pad_maximum_fusion.11), channel_id=1, source_target_pairs={{0,8},{1,9},{2,10},{3,11},{4,12},{5,13},{6,14},{7,15},{8,0},{9,1},... | collective-permute-start | bytes 393224 | tf_op jit(solution)/shard_map/ppermute | solution.py:48
  106.1 6.1 %collective-permute-start.3 = (bf16[64,1024]{1,0:T(8,128)(2,1)S(1)}, bf16[64,1024]{1,0:T(8,128)(2,1)S(1)}, u32[]{:S(2)}, u32[]{:S(2)}) collective-permute-start(bf16[64,1024]{1,0:T(8,128)(2,1)S(1)} %get-tuple-element.225), channel_id=1, source_target_pairs={{0,2},{1,3},{2,0},{3,1},{4,6},{5,7},{6,4},{7,5},{8,10},{9,11},{10,... | collective-permute-start | bytes 393224 | tf_op jit(solution)/shard_map/ppermute | solution.py:48
  112.2 1.9 collective-permute-start.6
  114.2 1.9 collective-permute-start.12
  116.1 17.9 %collective-permute-start.15 = (bf16[256,256]{1,0:T(8,128)(2,1)S(1)}, bf16[256,256]{1,0:T(8,128)(2,1)S(1)}, u32[]{:S(2)}, u32[]{:S(2)}) collective-permute-start(bf16[256,256]{1,0:T(8,128)(2,1)S(1)} %get-tuple-element.216), channel_id=1, source_target_pairs={{0,6},{1,7},{2,4},{3,5},{4,2},{5,3},{6,0},{7,1},{8,14},{9,15},{10,... | collective-permute-start | bytes 393224 | tf_op jit(solution)/shard_map/ppermute | solution.py:48
  134.1 19.0 %collective-permute-start.4 = (bf16[128,1024]{1,0:T(8,128)(2,1)S(1)}, bf16[128,1024]{1,0:T(8,128)(2,1)S(1)}, u32[]{:S(2)}, u32[]{:S(2)}) collective-permute-start(bf16[128,1024]{1,0:T(8,128)(2,1)S(1)} %pad_maximum_fusion.4), channel_id=1, source_target_pairs={{0,6},{1,7},{2,4},{3,5},{4,2},{5,3},{6,0},{7,1},{8,14},{9,15},{10,... | collective-permute-start | bytes 786440 | tf_op jit(solution)/shard_map/ppermute | solution.py:48
  153.2 6.1 %collective-permute-start.7 = (bf16[128,1024]{1,0:T(8,128)(2,1)S(1)}, bf16[128,1024]{1,0:T(8,128)(2,1)S(1)}, u32[]{:S(2)}, u32[]{:S(2)}) collective-permute-start(bf16[128,1024]{1,0:T(8,128)(2,1)S(1)} %pad_maximum_fusion.5), channel_id=1, source_target_pairs={{0,2},{1,3},{2,0},{3,1},{4,6},{5,7},{6,4},{7,5},{8,10},{9,11},{10,... | collective-permute-start | bytes 786440 | tf_op jit(solution)/shard_map/ppermute | solution.py:48
  159.4 1.9 collective-permute-start.13
  161.4 1.9 collective-permute-start.16
  163.5 1.9 collective-permute-start.5
  165.4 2.2 collective-permute-done.13
  167.8 18.3 %collective-permute-start.14 = (bf16[1024,256]{1,0:T(8,128)(2,1)S(1)}, bf16[1024,256]{1,0:T(8,128)(2,1)S(1)}, u32[]{:S(2)}, u32[]{:S(2)}) collective-permute-start(bf16[1024,256]{1,0:T(8,128)(2,1)S(1)} %pad_maximum_fusion.2), channel_id=1, source_target_pairs={{0,1},{1,0},{2,3},{3,2},{4,5},{5,4},{6,7},{7,6},{8,9},{9,8},{10,11... | collective-permute-start | bytes 1572872 | tf_op jit(solution)/shard_map/ppermute | solution.py:48
  186.2 19.0 %collective-permute-start.17 = (bf16[1024,256]{1,0:T(8,128)(2,1)S(1)}, bf16[1024,256]{1,0:T(8,128)(2,1)S(1)}, u32[]{:S(2)}, u32[]{:S(2)}) collective-permute-start(bf16[1024,256]{1,0:T(8,128)(2,1)S(1)} %pad_maximum_fusion.3), channel_id=1, source_target_pairs={{0,1},{1,0},{2,3},{3,2},{4,5},{5,4},{6,7},{7,6},{8,9},{9,8},{10,11... | collective-permute-start | bytes 1572872 | tf_op jit(solution)/shard_map/ppermute | solution.py:48
  205.3 2.1 collective-permute-start.8
  209.6 2.5 layer_up_0.3
  212.1 1.5 collective-permute-start.33
  213.6 2.5 layer_up_0.2
  216.1 1.3 collective-permute-start.18
  218.1 2.4 collective-permute-done.18.refs_1_
  221.2 0.7 collective-permute-start.35
  224.2 0.8 collective-permute-start.37
  225.1 0.7 collective-permute-start.22
  225.8 8.3 %collective-permute-start.25 = (bf16[128,512]{1,0:T(8,128)(2,1)S(1)}, bf16[128,512]{1,0:T(8,128)(2,1)S(1)}, u32[]{:S(2)}, u32[]{:S(2)}) collective-permute-start(bf16[128,512]{1,0:T(8,128)(2,1)S(1)} %copy-done.3), channel_id=1, source_target_pairs={{0,32},{1,33},{2,34},{3,35},{4,36},{5,37},{6,38},{7,39},{8,40},{9,... | collective-permute-start | bytes 393224 | tf_op jit(solution)/shard_map/ppermute | solution.py:48
  234.1 0.7 collective-permute-start.38
  235.5 10.0 %collective-permute-done.25 = bf16[128,512]{1,0:T(8,128)(2,1)S(1)} collective-permute-done((bf16[128,512]{1,0:T(8,128)(2,1)S(1)}, bf16[128,512]{1,0:T(8,128)(2,1)S(1)}, u32[]{:S(2)}, u32[]{:S(2)}) %collective-permute-start.25) | collective-permute-done | bytes 131104 | tf_op jit(solution)/shard_map/ppermute | solution.py:48
  248.0 0.7 collective-permute-start.26
  250.8 0.7 collective-permute-start.28
  251.7 0.7 collective-permute-start.43
  256.0 1.3 collective-permute-start.46
  257.3 1.3 collective-permute-start.32
  258.6 85.5 %collective-permute-done.46.refs_2_ = bf16[2,64,512]{2,1,0:T(8,128)(2,1)S(1)} collective-permute-done((bf16[2,64,512]{2,1,0:T(8,128)(2,1)S(1)}, bf16[2,64,512]{2,1,0:T(8,128)(2,1)S(1)}, u32[]{:S(2)}, u32[]{:S(2)}) %collective-permute-start.46) | collective-permute-done | bytes 131104 | tf_op jit(solution)/shard_map/ppermute | solution.py:48
  344.1 2.3 curvature_first.1
  346.4 3.5 collective-permute-done.32.refs_2_
  349.9 2.3 curvature_last.1
  352.3 1.9 collective-permute-start.47
  354.2 2.6 collective-permute-done.47
  357.1 18.7 %all_to_all.10 = bf16[4,64,2048]{2,1,0:T(8,128)(2,1)S(1)} all-to-all(bf16[4,64,2048]{2,1,0:T(8,128)(2,1)S(1)} %bitcast.68), channel_id=1, replica_groups=mesh['zh'=2,'x'=4,'b4'=2,'b2'=2,'b1'=2,'y'=4,'c'=2] {'y'}, dimensions={0} | all-to-all | bytes 2097152 | tf_op jit(solution)/shard_map/all_to_all | solution.py:400
  375.8 0.9 reduce_sum.23
  376.8 8.3 %all-to-all-start.1 = ((bf16[8,8,2048]{2,1,0:T(8,128)(2,1)}), bf16[8,8,2048]{2,1,0:T(8,128)(2,1)S(1)}, u32[]{:S(2)}, u32[]{:S(2)}) async-start(bf16[8,8,2048]{2,1,0:T(8,128)(2,1)} %bitcast.15), calls=%async_computation.1 | async-start | bytes 524288 | tf_op jit(solution)/shard_map/all_to_all | solution.py:402
  385.0 15.5 %all-to-all-done.1 = bf16[8,8,2048]{2,1,0:T(8,128)(2,1)S(1)} async-done(((bf16[8,8,2048]{2,1,0:T(8,128)(2,1)}), bf16[8,8,2048]{2,1,0:T(8,128)(2,1)S(1)}, u32[]{:S(2)}, u32[]{:S(2)}) %all-to-all-start.1) | async-done | bytes 262176 | tf_op jit(solution)/shard_map/all_to_all | solution.py:402
  400.6 1.4 bitcast_multiply_fusion
  (148 shorter events, 16.4 us)
Async XLA Ops:
  0.0 29.7 %collective-permute-start = (bf16[8,2048]{1,0:T(8,128)(2,1)}, bf16[8,2048]{1,0:T(8,128)(2,1)S(1)}, u32[]{:S(2)}, u32[]{:S(2)}) collective-permute-start(bf16[8,2048]{1,0:T(8,128)(2,1)} %bitcast.69), channel_id=1, source_target_pairs={{0,32},{1,33},{2,34},{3,35},{4,36},{5,37},{6,38},{7,39},{8,40},{9,... | collective-permute-start | bytes 98312 | tf_op jit(solution)/shard_map/ppermute | solution.py:48
  10.6 38.2 %collective-permute-start.9 = (bf16[32,512]{1,0:T(8,128)(2,1)S(1)}, bf16[32,512]{1,0:T(8,128)(2,1)S(1)}, u32[]{:S(2)}, u32[]{:S(2)}) collective-permute-start(bf16[32,512]{1,0:T(8,128)(2,1)S(1)} %convolution_bitcast_fusion.2), channel_id=1, source_target_pairs={{0,32},{1,33},{2,34},{3,35},{4,36},{5,37},{6,38},{7,39},{8,40},{9,... | collective-permute-start | bytes 98312 | tf_op jit(solution)/shard_map/ppermute | solution.py:48
  29.8 38.1 %collective-permute-start.1 = (bf16[16,2048]{1,0:T(8,128)(2,1)S(1)}, bf16[16,2048]{1,0:T(8,128)(2,1)S(1)}, u32[]{:S(2)}, u32[]{:S(2)}) collective-permute-start(bf16[16,2048]{1,0:T(8,128)(2,1)S(1)} %pad_maximum_fusion.12), channel_id=1, source_target_pairs={{0,16},{1,17},{2,18},{3,19},{4,20},{5,21},{6,22},{7,23},{8,24},{9,... | collective-permute-start | bytes 196616 | tf_op jit(solution)/shard_map/ppermute | solution.py:48
  48.8 38.1 %collective-permute-start.10 = (bf16[64,512]{1,0:T(8,128)(2,1)S(1)}, bf16[64,512]{1,0:T(8,128)(2,1)S(1)}, u32[]{:S(2)}, u32[]{:S(2)}) collective-permute-start(bf16[64,512]{1,0:T(8,128)(2,1)S(1)} %pad_maximum_fusion.13), channel_id=1, source_target_pairs={{0,16},{1,17},{2,18},{3,19},{4,20},{5,21},{6,22},{7,23},{8,24},{9,... | collective-permute-start | bytes 196616 | tf_op jit(solution)/shard_map/ppermute | solution.py:48
  67.9 38.1 %collective-permute-start.2 = (bf16[32,2048]{1,0:T(8,128)(2,1)S(1)}, bf16[32,2048]{1,0:T(8,128)(2,1)S(1)}, u32[]{:S(2)}, u32[]{:S(2)}) collective-permute-start(bf16[32,2048]{1,0:T(8,128)(2,1)S(1)} %pad_maximum_fusion.10), channel_id=1, source_target_pairs={{0,8},{1,9},{2,10},{3,11},{4,12},{5,13},{6,14},{7,15},{8,0},{9,1},... | collective-permute-start | bytes 393224 | tf_op jit(solution)/shard_map/ppermute | solution.py:48
  87.0 27.1 %collective-permute-start.11 = (bf16[128,512]{1,0:T(8,128)(2,1)S(1)}, bf16[128,512]{1,0:T(8,128)(2,1)S(1)}, u32[]{:S(2)}, u32[]{:S(2)}) collective-permute-start(bf16[128,512]{1,0:T(8,128)(2,1)S(1)} %pad_maximum_fusion.11), channel_id=1, source_target_pairs={{0,8},{1,9},{2,10},{3,11},{4,12},{5,13},{6,14},{7,15},{8,0},{9,1},... | collective-permute-start | bytes 393224 | tf_op jit(solution)/shard_map/ppermute | solution.py:48
  106.1 28.0 %collective-permute-start.3 = (bf16[64,1024]{1,0:T(8,128)(2,1)S(1)}, bf16[64,1024]{1,0:T(8,128)(2,1)S(1)}, u32[]{:S(2)}, u32[]{:S(2)}) collective-permute-start(bf16[64,1024]{1,0:T(8,128)(2,1)S(1)} %get-tuple-element.225), channel_id=1, source_target_pairs={{0,2},{1,3},{2,0},{3,1},{4,6},{5,7},{6,4},{7,5},{8,10},{9,11},{10,... | collective-permute-start | bytes 393224 | tf_op jit(solution)/shard_map/ppermute | solution.py:48
  112.2 41.0 %collective-permute-start.6 = (bf16[64,1024]{1,0:T(8,128)(2,1)S(1)}, bf16[64,1024]{1,0:T(8,128)(2,1)S(1)}, u32[]{:S(2)}, u32[]{:S(2)}) collective-permute-start(bf16[64,1024]{1,0:T(8,128)(2,1)S(1)} %get-tuple-element.226), channel_id=1, source_target_pairs={{0,6},{1,7},{2,4},{3,5},{4,2},{5,3},{6,0},{7,1},{8,14},{9,15},{10,... | collective-permute-start | bytes 393224 | tf_op jit(solution)/shard_map/ppermute | solution.py:48
  114.2 45.1 %collective-permute-start.12 = (bf16[256,256]{1,0:T(8,128)(2,1)S(1)}, bf16[256,256]{1,0:T(8,128)(2,1)S(1)}, u32[]{:S(2)}, u32[]{:S(2)}) collective-permute-start(bf16[256,256]{1,0:T(8,128)(2,1)S(1)} %get-tuple-element.215), channel_id=1, source_target_pairs={{0,2},{1,3},{2,0},{3,1},{4,6},{5,7},{6,4},{7,5},{8,10},{9,11},{10,... | collective-permute-start | bytes 393224 | tf_op jit(solution)/shard_map/ppermute | solution.py:48
  116.1 45.2 %collective-permute-start.15 = (bf16[256,256]{1,0:T(8,128)(2,1)S(1)}, bf16[256,256]{1,0:T(8,128)(2,1)S(1)}, u32[]{:S(2)}, u32[]{:S(2)}) collective-permute-start(bf16[256,256]{1,0:T(8,128)(2,1)S(1)} %get-tuple-element.216), channel_id=1, source_target_pairs={{0,6},{1,7},{2,4},{3,5},{4,2},{5,3},{6,0},{7,1},{8,14},{9,15},{10,... | collective-permute-start | bytes 393224 | tf_op jit(solution)/shard_map/ppermute | solution.py:48
  134.1 29.2 %collective-permute-start.4 = (bf16[128,1024]{1,0:T(8,128)(2,1)S(1)}, bf16[128,1024]{1,0:T(8,128)(2,1)S(1)}, u32[]{:S(2)}, u32[]{:S(2)}) collective-permute-start(bf16[128,1024]{1,0:T(8,128)(2,1)S(1)} %pad_maximum_fusion.4), channel_id=1, source_target_pairs={{0,6},{1,7},{2,4},{3,5},{4,2},{5,3},{6,0},{7,1},{8,14},{9,15},{10,... | collective-permute-start | bytes 786440 | tf_op jit(solution)/shard_map/ppermute | solution.py:48
  153.2 52.0 %collective-permute-start.7 = (bf16[128,1024]{1,0:T(8,128)(2,1)S(1)}, bf16[128,1024]{1,0:T(8,128)(2,1)S(1)}, u32[]{:S(2)}, u32[]{:S(2)}) collective-permute-start(bf16[128,1024]{1,0:T(8,128)(2,1)S(1)} %pad_maximum_fusion.5), channel_id=1, source_target_pairs={{0,2},{1,3},{2,0},{3,1},{4,6},{5,7},{6,4},{7,5},{8,10},{9,11},{10,... | collective-permute-start | bytes 786440 | tf_op jit(solution)/shard_map/ppermute | solution.py:48
  159.4 8.3 %collective-permute-start.13 = (bf16[512,256]{1,0:T(8,128)(2,1)S(1)}, bf16[512,256]{1,0:T(8,128)(2,1)S(1)}, u32[]{:S(2)}, u32[]{:S(2)}) collective-permute-start(bf16[512,256]{1,0:T(8,128)(2,1)S(1)} %pad_maximum_fusion.6), channel_id=1, source_target_pairs={{0,6},{1,7},{2,4},{3,5},{4,2},{5,3},{6,0},{7,1},{8,14},{9,15},{10,... | collective-permute-start | bytes 786440 | tf_op jit(solution)/shard_map/ppermute | solution.py:48
  161.4 24.7 %collective-permute-start.16 = (bf16[512,256]{1,0:T(8,128)(2,1)S(1)}, bf16[512,256]{1,0:T(8,128)(2,1)S(1)}, u32[]{:S(2)}, u32[]{:S(2)}) collective-permute-start(bf16[512,256]{1,0:T(8,128)(2,1)S(1)} %pad_maximum_fusion.7), channel_id=1, source_target_pairs={{0,2},{1,3},{2,0},{3,1},{4,6},{5,7},{6,4},{7,5},{8,10},{9,11},{10,... | collective-permute-start | bytes 786440 | tf_op jit(solution)/shard_map/ppermute | solution.py:48
  163.5 44.8 %collective-permute-start.5 = (bf16[256,1024]{1,0:T(8,128)(2,1)S(1)}, bf16[256,1024]{1,0:T(8,128)(2,1)S(1)}, u32[]{:S(2)}, u32[]{:S(2)}) collective-permute-start(bf16[256,1024]{1,0:T(8,128)(2,1)S(1)} %pad_maximum_fusion), channel_id=1, source_target_pairs={{0,1},{1,0},{2,3},{3,2},{4,5},{5,4},{6,7},{7,6},{8,9},{9,8},{10,11... | collective-permute-start | bytes 1572872 | tf_op jit(solution)/shard_map/ppermute | solution.py:48
  167.8 39.6 %collective-permute-start.14 = (bf16[1024,256]{1,0:T(8,128)(2,1)S(1)}, bf16[1024,256]{1,0:T(8,128)(2,1)S(1)}, u32[]{:S(2)}, u32[]{:S(2)}) collective-permute-start(bf16[1024,256]{1,0:T(8,128)(2,1)S(1)} %pad_maximum_fusion.2), channel_id=1, source_target_pairs={{0,1},{1,0},{2,3},{3,2},{4,5},{5,4},{6,7},{7,6},{8,9},{9,8},{10,11... | collective-permute-start | bytes 1572872 | tf_op jit(solution)/shard_map/ppermute | solution.py:48
  186.2 21.4 %collective-permute-start.17 = (bf16[1024,256]{1,0:T(8,128)(2,1)S(1)}, bf16[1024,256]{1,0:T(8,128)(2,1)S(1)}, u32[]{:S(2)}, u32[]{:S(2)}) collective-permute-start(bf16[1024,256]{1,0:T(8,128)(2,1)S(1)} %pad_maximum_fusion.3), channel_id=1, source_target_pairs={{0,1},{1,0},{2,3},{3,2},{4,5},{5,4},{6,7},{7,6},{8,9},{9,8},{10,11... | collective-permute-start | bytes 1572872 | tf_op jit(solution)/shard_map/ppermute | solution.py:48
  205.3 3.8 collective-permute-start.8
  212.1 5.3 %collective-permute-start.33 = (bf16[2,64,512]{2,1,0:T(8,128)(2,1)S(1)}, bf16[2,64,512]{2,1,0:T(8,128)(2,1)S(1)}, u32[]{:S(2)}, u32[]{:S(2)}) collective-permute-start(bf16[2,64,512]{2,1,0:T(8,128)(2,1)S(1)} %get-tuple-element.144), channel_id=1, source_target_pairs={{0,64},{1,65},{2,66},{3,67},{4,68},{5,69},{6,70},{7,71},{8,72},{9,... | collective-permute-start | bytes 393224 | tf_op jit(solution)/shard_map/ppermute | solution.py:48
  216.1 4.4 %collective-permute-start.18 = (bf16[2,64,512]{2,1,0:T(8,128)(2,1)S(1)}, bf16[2,64,512]{2,1,0:T(8,128)(2,1)S(1)}, u32[]{:S(2)}, u32[]{:S(2)}) collective-permute-start(bf16[2,64,512]{2,1,0:T(8,128)(2,1)S(1)} %get-tuple-element.99), channel_id=1, source_target_pairs={{0,64},{1,65},{2,66},{3,67},{4,68},{5,69},{6,70},{7,71},{8,72},{9,... | collective-permute-start | bytes 393224 | tf_op jit(solution)/shard_map/ppermute | solution.py:48
  217.5 3.7 collective-permute-start.34
  221.2 1.4 collective-permute-start.35
  221.9 1.4 collective-permute-start.20
  222.6 1.4 collective-permute-start.36
  223.3 1.7 collective-permute-start.21
  224.2 9.8 %collective-permute-start.37 = (bf16[2,64,512]{2,1,0:T(8,128)(2,1)S(1)}, bf16[2,64,512]{2,1,0:T(8,128)(2,1)S(1)}, u32[]{:S(2)}, u32[]{:S(2)}) collective-permute-start(bf16[2,64,512]{2,1,0:T(8,128)(2,1)S(1)} %get-tuple-element.148), channel_id=1, source_target_pairs={{256,320},{257,321},{258,322},{259,323},{260,324},{261,325},{262,3... | collective-permute-start | bytes 393224 | tf_op jit(solution)/shard_map/ppermute | solution.py:48
  225.1 9.7 %collective-permute-start.22 = (bf16[2,64,512]{2,1,0:T(8,128)(2,1)S(1)}, bf16[2,64,512]{2,1,0:T(8,128)(2,1)S(1)}, u32[]{:S(2)}, u32[]{:S(2)}) collective-permute-start(bf16[2,64,512]{2,1,0:T(8,128)(2,1)S(1)} %get-tuple-element.103), channel_id=1, source_target_pairs={{256,320},{257,321},{258,322},{259,323},{260,324},{261,325},{262,3... | collective-permute-start | bytes 393224 | tf_op jit(solution)/shard_map/ppermute | solution.py:48
  225.8 19.7 %collective-permute-start.25 = (bf16[128,512]{1,0:T(8,128)(2,1)S(1)}, bf16[128,512]{1,0:T(8,128)(2,1)S(1)}, u32[]{:S(2)}, u32[]{:S(2)}) collective-permute-start(bf16[128,512]{1,0:T(8,128)(2,1)S(1)} %copy-done.3), channel_id=1, source_target_pairs={{0,32},{1,33},{2,34},{3,35},{4,36},{5,37},{6,38},{7,39},{8,40},{9,... | collective-permute-start | bytes 393224 | tf_op jit(solution)/shard_map/ppermute | solution.py:48
  234.1 11.7 %collective-permute-start.38 = (bf16[2,64,512]{2,1,0:T(8,128)(2,1)S(1)}, bf16[2,64,512]{2,1,0:T(8,128)(2,1)S(1)}, u32[]{:S(2)}, u32[]{:S(2)}) collective-permute-start(bf16[2,64,512]{2,1,0:T(8,128)(2,1)S(1)} %get-tuple-element.149), channel_id=1, source_target_pairs={{320,384},{321,385},{322,386},{323,387},{324,388},{325,389},{326,3... | collective-permute-start | bytes 393224 | tf_op jit(solution)/shard_map/ppermute | solution.py:48
  234.8 11.7 %collective-permute-start.23 = (bf16[2,64,512]{2,1,0:T(8,128)(2,1)S(1)}, bf16[2,64,512]{2,1,0:T(8,128)(2,1)S(1)}, u32[]{:S(2)}, u32[]{:S(2)}) collective-permute-start(bf16[2,64,512]{2,1,0:T(8,128)(2,1)S(1)} %get-tuple-element.104), channel_id=1, source_target_pairs={{320,384},{321,385},{322,386},{323,387},{324,388},{325,389},{326,3... | collective-permute-start | bytes 393224 | tf_op jit(solution)/shard_map/ppermute | solution.py:48
  245.8 1.4 collective-permute-start.39
  246.5 1.4 collective-permute-start.24
  247.3 1.4 collective-permute-start.40
  248.0 1.4 collective-permute-start.26
  248.7 1.4 collective-permute-start.41
  249.4 1.4 collective-permute-start.27
  250.1 1.4 collective-permute-start.42
  250.8 1.6 collective-permute-start.28
  251.7 1.4 collective-permute-start.43
  252.5 1.4 collective-permute-start.29
  253.2 1.4 collective-permute-start.44
  253.9 1.4 collective-permute-start.30
  254.6 1.4 collective-permute-start.45
  255.3 2.0 collective-permute-start.31
  256.0 88.1 %collective-permute-start.46 = (bf16[2,64,512]{2,1,0:T(8,128)(2,1)S(1)}, bf16[2,64,512]{2,1,0:T(8,128)(2,1)S(1)}, u32[]{:S(2)}, u32[]{:S(2)}) collective-permute-start(bf16[2,64,512]{2,1,0:T(8,128)(2,1)S(1)} %get-tuple-element.179), channel_id=1, source_target_pairs={{64,0},{65,1},{66,2},{67,3},{68,4},{69,5},{70,6},{71,7},{72,8},{73... | collective-permute-start | bytes 393224 | tf_op jit(solution)/shard_map/ppermute | solution.py:48
  257.3 92.6 %collective-permute-start.32 = (bf16[2,64,512]{2,1,0:T(8,128)(2,1)S(1)}, bf16[2,64,512]{2,1,0:T(8,128)(2,1)S(1)}, u32[]{:S(2)}, u32[]{:S(2)}) collective-permute-start(bf16[2,64,512]{2,1,0:T(8,128)(2,1)S(1)} %get-tuple-element.134), channel_id=1, source_target_pairs={{64,0},{65,1},{66,2},{67,3},{68,4},{69,5},{70,6},{71,7},{72,8},{73... | collective-permute-start | bytes 393224 | tf_op jit(solution)/shard_map/ppermute | solution.py:48
  352.3 4.6 %collective-permute-start.47 = (bf16[256,2048]{1,0:T(8,128)(2,1)S(1)}, bf16[256,2048]{1,0:T(8,128)(2,1)S(1)}, u32[]{:S(2)}, u32[]{:S(2)}) collective-permute-start(bf16[256,2048]{1,0:T(8,128)(2,1)S(1)} %get-tuple-element.192), channel_id=1, source_target_pairs={{0,1},{1,0},{2,3},{3,2},{4,5},{5,4},{6,7},{7,6},{8,9},{9,8},{10,11... | collective-permute-start | bytes 3145736 | tf_op jit(solution)/shard_map/ppermute | solution.py:48
  376.8 23.8 %all-to-all-start.1 = ((bf16[8,8,2048]{2,1,0:T(8,128)(2,1)}), bf16[8,8,2048]{2,1,0:T(8,128)(2,1)S(1)}, u32[]{:S(2)}, u32[]{:S(2)}) async-start(bf16[8,8,2048]{2,1,0:T(8,128)(2,1)} %bitcast.15), calls=%async_computation.1 | async-start | bytes 524288 | tf_op jit(solution)/shard_map/all_to_all | solution.py:402
  (5 other events, 77.2 us)

commit v3 on v2

--- a/solution.py
+++ b/solution.py
@@ -52,6 +52,10 @@
     return (zh, x, 1 - b4, b2, b1, y, c)
 
 
+def goal_route(zh, x, b4, b2, b1, y, c):
+    return (zh, x, 1 - b4, b2, b1, y, c) if (zh, x) == (1, 3) else None
+
+
 def swap_b2(zh, x, b4, b2, b1, y, c):
     return (zh, x, b4, 1 - b2, b1, y, c)
 
@@ -74,10 +78,10 @@
 
 def up_from(section):
     def route(zh, x, b4, b2, b1, y, c):
-        if zh * 4 + x != section:
+        if x != section % 4 or (x == 3 and zh == 1):
             return None
         if x == 3:
-            return (zh + 1, 0, 1 - b4, b2, b1, y, c)
+            return (1, 0, 1 - b4, b2, b1, y, c)
         return (zh, x + 1, b4, b2, b1, y, c)
 
     return route
@@ -85,10 +89,10 @@
 
 def down_from(section):
     def route(zh, x, b4, b2, b1, y, c):
-        if zh * 4 + x != section:
+        if x != section % 4 or (x == 0 and zh == 0):
             return None
         if x == 0:
-            return (zh - 1, 3, 1 - b4, b2, b1, y, c)
+            return (0, 3, 1 - b4, b2, b1, y, c)
         return (zh, x - 1, b4, b2, b1, y, c)
 
     return route
@@ -121,14 +125,8 @@
         ],
         axis=0,
     )
-    core = lax.axis_index("c")
-    return jnp.concatenate(
-        [
-            merged(left_four, routed(left_four, swap_core), core),
-            merged(right_four, routed(right_four, swap_core), core),
-        ],
-        axis=1,
-    )
+    half = jnp.concatenate([left_four, right_four], axis=1)
+    return merged(half, routed(half, swap_core), lax.axis_index("c"))
 
 
 def feature_order():
@@ -366,7 +364,7 @@
     )
     probe = lax.dot_general(order, probes[0], CONTRACT_FIRST, preferred_element_type=jnp.bfloat16)
     fresh = jnp.dot(inputs, order)
-    goal = jnp.dot(routed(targets, swap_b4), order)
+    goal = jnp.dot(routed(targets, goal_route), order)
     pairs, goals, kept, grads = [], [], [], []
     for micro in range(MICRO):
         rows = slice(micro * ROWS, (micro + 1) * ROWS)

time: 403 us -> 267 us (0.66)
  starting transfers between devices: 239 us -> 97.1 us
  other arithmetic: 5.03 us -> 9.12 us
    ppermute x48 -> x46, starting transfers between devices: 231 us -> 90.1 us  [routed(): return lax.ppermute(value, NAMES, pairs)]
    ppermute x48 -> x46, waiting for transfers between devices: 107 us -> 107 us  [routed(): return lax.ppermute(value, NAMES, pairs)]
  transfers between devices with their start and end apart: 49 -> 47, of which waited for: 8 -> 13; matrix products, arithmetic and copies ran while one was open for 2% -> 4% of each run, Pallas kernels for 1% -> 2%
where the time goes in v3:
time: 267 us; the launch traced here: 265 us
  waiting for transfers between devices  122 us (46%)
  starting transfers between devices  97.1 us (36%)
  blocking collectives  19.3 us (7%)
  Pallas kernels  10.1 us (4%)
  other arithmetic  9.12 us (3%)
  matrix products  4.44 us (2%)
    ppermute x46, waiting for transfers between devices, routed(): return lax.ppermute(value, NAMES, pairs)  107 us
    ppermute x46, starting transfers between devices, routed(): return lax.ppermute(value, NAMES, pairs)  90.1 us
    all_to_all x1, blocking collectives, shards(): lax.all_to_all(summed.reshape(4, 64, HIDDEN), 'y', 0, 0, tiled=True)  19.3 us
    all_to_all x1, waiting for transfers between devices, shards(): lax.all_to_all(summed.reshape(8, 8, HIDDEN), ('b1', 'b2', 'b4'), 0, 0, ti...  15.5 us
    all_to_all x1, starting transfers between devices, shards(): lax.all_to_all(summed.reshape(8, 8, HIDDEN), ('b1', 'b2', 'b4'), 0, 0, ti...  6.98 us
    pallas_call x16, Pallas kernels, forward_call(): pl.pallas_call(functools.partial(forward_kernel, tick), out_shape=[PAIR,...  5.35 us
  transfers between devices with their start and end apart: 47, of which 13 were waited for; matrix products, arithmetic and copies ran while one was open for 4% of the time, Pallas kernels for 2%

profile of v3, /device:TPU:8, one launch (start us, length us, event | category | flops | bytes accessed | tf_op | source)
XLA Modules:
  0.0 265.5 jit_solution(15145671312615037424)
XLA Ops:
  0.0 9.2 %collective-permute-start = (bf16[8,2048]{1,0:T(8,128)(2,1)}, bf16[8,2048]{1,0:T(8,128)(2,1)S(1)}, u32[]{:S(2)}, u32[]{:S(2)}) collective-permute-start(bf16[8,2048]{1,0:T(8,128)(2,1)} %bitcast.69), channel_id=1, source_target_pairs={{0,32},{1,33},{2,34},{3,35},{4,36},{5,37},{6,38},{7,39},{8,40},{9,... | collective-permute-start | bytes 98312 | tf_op jit(solution)/shard_map/ppermute | solution.py:48
  9.6 1.0 convolution_bitcast_fusion.2
  10.6 1.9 collective-permute-start.8
  13.6 5.2 %collective-permute-start.1 = (bf16[16,2048]{1,0:T(8,128)(2,1)S(1)}, bf16[16,2048]{1,0:T(8,128)(2,1)S(1)}, u32[]{:S(2)}, u32[]{:S(2)}) collective-permute-start(bf16[16,2048]{1,0:T(8,128)(2,1)S(1)} %pad_maximum_fusion.10), channel_id=1, source_target_pairs={{0,16},{1,17},{2,18},{3,19},{4,20},{5,21},{6,22},{7,23},{8,24},{9,... | collective-permute-start | bytes 196616 | tf_op jit(solution)/shard_map/ppermute | solution.py:48
  18.8 1.8 collective-permute-done.8
  20.7 5.1 %collective-permute-start.9 = (bf16[64,512]{1,0:T(8,128)(2,1)S(1)}, bf16[64,512]{1,0:T(8,128)(2,1)S(1)}, u32[]{:S(2)}, u32[]{:S(2)}) collective-permute-start(bf16[64,512]{1,0:T(8,128)(2,1)S(1)} %pad_maximum_fusion.11), channel_id=1, source_target_pairs={{0,16},{1,17},{2,18},{3,19},{4,20},{5,21},{6,22},{7,23},{8,24},{9,... | collective-permute-start | bytes 196616 | tf_op jit(solution)/shard_map/ppermute | solution.py:48
  25.8 3.5 %collective-permute-start.2 = (bf16[32,2048]{1,0:T(8,128)(2,1)S(1)}, bf16[32,2048]{1,0:T(8,128)(2,1)S(1)}, u32[]{:S(2)}, u32[]{:S(2)}) collective-permute-start(bf16[32,2048]{1,0:T(8,128)(2,1)S(1)} %pad_maximum_fusion.8), channel_id=1, source_target_pairs={{0,8},{1,9},{2,10},{3,11},{4,12},{5,13},{6,14},{7,15},{8,0},{9,1},... | collective-permute-start | bytes 393224 | tf_op jit(solution)/shard_map/ppermute | solution.py:48
  29.5 2.8 %collective-permute-start.10 = (bf16[128,512]{1,0:T(8,128)(2,1)S(1)}, bf16[128,512]{1,0:T(8,128)(2,1)S(1)}, u32[]{:S(2)}, u32[]{:S(2)}) collective-permute-start(bf16[128,512]{1,0:T(8,128)(2,1)S(1)} %pad_maximum_fusion.9), channel_id=1, source_target_pairs={{0,8},{1,9},{2,10},{3,11},{4,12},{5,13},{6,14},{7,15},{8,0},{9,1},... | collective-permute-start | bytes 393224 | tf_op jit(solution)/shard_map/ppermute | solution.py:48
  32.3 1.4 collective-permute-done.2
  33.7 2.4 collective-permute-start.3
  36.1 4.3 %collective-permute-start.5 = (bf16[64,1024]{1,0:T(8,128)(2,1)S(1)}, bf16[64,1024]{1,0:T(8,128)(2,1)S(1)}, u32[]{:S(2)}, u32[]{:S(2)}) collective-permute-start(bf16[64,1024]{1,0:T(8,128)(2,1)S(1)} %get-tuple-element.222), channel_id=1, source_target_pairs={{0,6},{1,7},{2,4},{3,5},{4,2},{5,3},{6,0},{7,1},{8,14},{9,15},{10,... | collective-permute-start | bytes 393224 | tf_op jit(solution)/shard_map/ppermute | solution.py:48
  40.5 3.3 %collective-permute-start.11 = (bf16[256,256]{1,0:T(8,128)(2,1)S(1)}, bf16[256,256]{1,0:T(8,128)(2,1)S(1)}, u32[]{:S(2)}, u32[]{:S(2)}) collective-permute-start(bf16[256,256]{1,0:T(8,128)(2,1)S(1)} %get-tuple-element.211), channel_id=1, source_target_pairs={{0,2},{1,3},{2,0},{3,1},{4,6},{5,7},{6,4},{7,5},{8,10},{9,11},{10,... | collective-permute-start | bytes 393224 | tf_op jit(solution)/shard_map/ppermute | solution.py:48
  43.8 2.4 collective-permute-start.13
  46.2 3.5 %collective-permute-start.4 = (bf16[128,1024]{1,0:T(8,128)(2,1)S(1)}, bf16[128,1024]{1,0:T(8,128)(2,1)S(1)}, u32[]{:S(2)}, u32[]{:S(2)}) collective-permute-start(bf16[128,1024]{1,0:T(8,128)(2,1)S(1)} %pad_maximum_fusion.2), channel_id=1, source_target_pairs={{0,6},{1,7},{2,4},{3,5},{4,2},{5,3},{6,0},{7,1},{8,14},{9,15},{10,... | collective-permute-start | bytes 786440 | tf_op jit(solution)/shard_map/ppermute | solution.py:48
  49.8 2.4 collective-permute-start.12
  52.2 4.0 %collective-permute-start.14 = (bf16[512,256]{1,0:T(8,128)(2,1)S(1)}, bf16[512,256]{1,0:T(8,128)(2,1)S(1)}, u32[]{:S(2)}, u32[]{:S(2)}) collective-permute-start(bf16[512,256]{1,0:T(8,128)(2,1)S(1)} %pad_maximum_fusion.5), channel_id=1, source_target_pairs={{0,2},{1,3},{2,0},{3,1},{4,6},{5,7},{6,4},{7,5},{8,10},{9,11},{10,... | collective-permute-start | bytes 786440 | tf_op jit(solution)/shard_map/ppermute | solution.py:48
  56.3 1.9 collective-permute-start.6
  58.2 2.4 collective-permute-done.14
  60.8 1.1 maximum_maximum_fusion.1
  61.9 1.9 collective-permute-start.15
  64.7 1.1 maximum_maximum_fusion
  65.8 1.9 collective-permute-start.7
  69.2 2.9 %fusion.refs_3_ = bf16[512,2048]{1,0:T(8,128)(2,1)S(1)} fusion(pred[512,512]{1,0:T(32,128)(4,1)S(1)} %fusion.9, bf16[1,512,2048]{2,1,0:T(8,128)(2,1)} %param.9), kind=kOutput, calls=%fused_computation.2 | convolution fusion | flops 1073741824 | bytes 4456448 | tf_op jit(solution)/shard_map/dot_general | solution.py:365
  72.9 1.8 broadcast_select_fusion.3
  74.9 2.5 layer_up_0.3
  77.5 1.5 collective-permute-start.31
  79.0 2.5 layer_up_0.2
  81.5 1.3 collective-permute-start.16
  83.5 2.7 %collective-permute-done.16.refs_1_ = bf16[2,64,512]{2,1,0:T(8,128)(2,1)S(1)} collective-permute-done((bf16[2,64,512]{2,1,0:T(8,128)(2,1)S(1)}, bf16[2,64,512]{2,1,0:T(8,128)(2,1)S(1)}, u32[]{:S(2)}, u32[]{:S(2)}) %collective-permute-start.16) | collective-permute-done | bytes 131104 | tf_op jit(solution)/shard_map/ppermute | solution.py:48
  90.0 9.3 %collective-permute-start.35 = (bf16[2,64,512]{2,1,0:T(8,128)(2,1)S(1)}, bf16[2,64,512]{2,1,0:T(8,128)(2,1)S(1)}, u32[]{:S(2)}, u32[]{:S(2)}) collective-permute-start(bf16[2,64,512]{2,1,0:T(8,128)(2,1)S(1)} %get-tuple-element.148), channel_id=1, source_target_pairs={{0,64},{1,65},{2,66},{3,67},{4,68},{5,69},{6,70},{7,71},{8,72},{9,... | collective-permute-start | bytes 393224 | tf_op jit(solution)/shard_map/ppermute | solution.py:48
  99.3 1.3 collective-permute-start.20
  101.3 1.5 collective-permute-done.35.refs_1_
  109.5 1.3 collective-permute-start.40
  110.8 1.3 collective-permute-start.26
  112.1 40.5 %collective-permute-done.40.refs_1_ = bf16[2,64,512]{2,1,0:T(8,128)(2,1)S(1)} collective-permute-done((bf16[2,64,512]{2,1,0:T(8,128)(2,1)S(1)}, bf16[2,64,512]{2,1,0:T(8,128)(2,1)S(1)}, u32[]{:S(2)}, u32[]{:S(2)}) %collective-permute-start.40) | collective-permute-done | bytes 131104 | tf_op jit(solution)/shard_map/ppermute | solution.py:48
  157.6 1.3 collective-permute-start.44
  158.9 1.3 collective-permute-start.30
  160.2 49.8 %collective-permute-done.44.refs_2_ = bf16[2,64,512]{2,1,0:T(8,128)(2,1)S(1)} collective-permute-done((bf16[2,64,512]{2,1,0:T(8,128)(2,1)S(1)}, bf16[2,64,512]{2,1,0:T(8,128)(2,1)S(1)}, u32[]{:S(2)}, u32[]{:S(2)}) %collective-permute-start.44) | collective-permute-done | bytes 131104 | tf_op jit(solution)/shard_map/ppermute | solution.py:48
  210.0 2.3 curvature_first.1
  212.4 1.7 collective-permute-done.30.refs_2_
  214.1 2.3 curvature_last.1
  216.4 1.9 collective-permute-start.45
  218.4 2.6 collective-permute-done.45
  221.3 19.3 %all_to_all.10 = bf16[4,64,2048]{2,1,0:T(8,128)(2,1)S(1)} all-to-all(bf16[4,64,2048]{2,1,0:T(8,128)(2,1)S(1)} %bitcast.68), channel_id=1, replica_groups=mesh['zh'=2,'x'=4,'b4'=2,'b2'=2,'b1'=2,'y'=4,'c'=2] {'y'}, dimensions={0} | all-to-all | bytes 2097152 | tf_op jit(solution)/shard_map/all_to_all | solution.py:398
  240.6 0.9 reduce_sum.23
  241.5 7.0 %all-to-all-start.1 = ((bf16[8,8,2048]{2,1,0:T(8,128)(2,1)}), bf16[8,8,2048]{2,1,0:T(8,128)(2,1)S(1)}, u32[]{:S(2)}, u32[]{:S(2)}) async-start(bf16[8,8,2048]{2,1,0:T(8,128)(2,1)} %bitcast.15), calls=%async_computation.1 | async-start | bytes 524288 | tf_op jit(solution)/shard_map/all_to_all | solution.py:400
  248.5 15.5 %all-to-all-done.1 = bf16[8,8,2048]{2,1,0:T(8,128)(2,1)S(1)} async-done(((bf16[8,8,2048]{2,1,0:T(8,128)(2,1)}), bf16[8,8,2048]{2,1,0:T(8,128)(2,1)S(1)}, u32[]{:S(2)}, u32[]{:S(2)}) %all-to-all-start.1) | async-done | bytes 262176 | tf_op jit(solution)/shard_map/all_to_all | solution.py:400
  264.1 1.4 bitcast_multiply_fusion
  (140 shorter events, 21.9 us)
Async XLA Ops:
  0.0 12.8 %collective-permute-start = (bf16[8,2048]{1,0:T(8,128)(2,1)}, bf16[8,2048]{1,0:T(8,128)(2,1)S(1)}, u32[]{:S(2)}, u32[]{:S(2)}) collective-permute-start(bf16[8,2048]{1,0:T(8,128)(2,1)} %bitcast.69), channel_id=1, source_target_pairs={{0,32},{1,33},{2,34},{3,35},{4,36},{5,37},{6,38},{7,39},{8,40},{9,... | collective-permute-start | bytes 98312 | tf_op jit(solution)/shard_map/ppermute | solution.py:48
  10.6 10.1 %collective-permute-start.8 = (bf16[32,512]{1,0:T(8,128)(2,1)S(1)}, bf16[32,512]{1,0:T(8,128)(2,1)S(1)}, u32[]{:S(2)}, u32[]{:S(2)}) collective-permute-start(bf16[32,512]{1,0:T(8,128)(2,1)S(1)} %convolution_bitcast_fusion.2), channel_id=1, source_target_pairs={{0,32},{1,33},{2,34},{3,35},{4,36},{5,37},{6,38},{7,39},{8,40},{9,... | collective-permute-start | bytes 98312 | tf_op jit(solution)/shard_map/ppermute | solution.py:48
  13.6 12.2 %collective-permute-start.1 = (bf16[16,2048]{1,0:T(8,128)(2,1)S(1)}, bf16[16,2048]{1,0:T(8,128)(2,1)S(1)}, u32[]{:S(2)}, u32[]{:S(2)}) collective-permute-start(bf16[16,2048]{1,0:T(8,128)(2,1)S(1)} %pad_maximum_fusion.10), channel_id=1, source_target_pairs={{0,16},{1,17},{2,18},{3,19},{4,20},{5,21},{6,22},{7,23},{8,24},{9,... | collective-permute-start | bytes 196616 | tf_op jit(solution)/shard_map/ppermute | solution.py:48
  20.7 8.7 %collective-permute-start.9 = (bf16[64,512]{1,0:T(8,128)(2,1)S(1)}, bf16[64,512]{1,0:T(8,128)(2,1)S(1)}, u32[]{:S(2)}, u32[]{:S(2)}) collective-permute-start(bf16[64,512]{1,0:T(8,128)(2,1)S(1)} %pad_maximum_fusion.11), channel_id=1, source_target_pairs={{0,16},{1,17},{2,18},{3,19},{4,20},{5,21},{6,22},{7,23},{8,24},{9,... | collective-permute-start | bytes 196616 | tf_op jit(solution)/shard_map/ppermute | solution.py:48
  25.8 7.8 %collective-permute-start.2 = (bf16[32,2048]{1,0:T(8,128)(2,1)S(1)}, bf16[32,2048]{1,0:T(8,128)(2,1)S(1)}, u32[]{:S(2)}, u32[]{:S(2)}) collective-permute-start(bf16[32,2048]{1,0:T(8,128)(2,1)S(1)} %pad_maximum_fusion.8), channel_id=1, source_target_pairs={{0,8},{1,9},{2,10},{3,11},{4,12},{5,13},{6,14},{7,15},{8,0},{9,1},... | collective-permute-start | bytes 393224 | tf_op jit(solution)/shard_map/ppermute | solution.py:48
  29.5 11.0 %collective-permute-start.10 = (bf16[128,512]{1,0:T(8,128)(2,1)S(1)}, bf16[128,512]{1,0:T(8,128)(2,1)S(1)}, u32[]{:S(2)}, u32[]{:S(2)}) collective-permute-start(bf16[128,512]{1,0:T(8,128)(2,1)S(1)} %pad_maximum_fusion.9), channel_id=1, source_target_pairs={{0,8},{1,9},{2,10},{3,11},{4,12},{5,13},{6,14},{7,15},{8,0},{9,1},... | collective-permute-start | bytes 393224 | tf_op jit(solution)/shard_map/ppermute | solution.py:48
  33.7 12.4 %collective-permute-start.3 = (bf16[64,1024]{1,0:T(8,128)(2,1)S(1)}, bf16[64,1024]{1,0:T(8,128)(2,1)S(1)}, u32[]{:S(2)}, u32[]{:S(2)}) collective-permute-start(bf16[64,1024]{1,0:T(8,128)(2,1)S(1)} %get-tuple-element.221), channel_id=1, source_target_pairs={{0,2},{1,3},{2,0},{3,1},{4,6},{5,7},{6,4},{7,5},{8,10},{9,11},{10,... | collective-permute-start | bytes 393224 | tf_op jit(solution)/shard_map/ppermute | solution.py:48
  36.1 20.1 %collective-permute-start.5 = (bf16[64,1024]{1,0:T(8,128)(2,1)S(1)}, bf16[64,1024]{1,0:T(8,128)(2,1)S(1)}, u32[]{:S(2)}, u32[]{:S(2)}) collective-permute-start(bf16[64,1024]{1,0:T(8,128)(2,1)S(1)} %get-tuple-element.222), channel_id=1, source_target_pairs={{0,6},{1,7},{2,4},{3,5},{4,2},{5,3},{6,0},{7,1},{8,14},{9,15},{10,... | collective-permute-start | bytes 393224 | tf_op jit(solution)/shard_map/ppermute | solution.py:48
  40.5 9.2 %collective-permute-start.11 = (bf16[256,256]{1,0:T(8,128)(2,1)S(1)}, bf16[256,256]{1,0:T(8,128)(2,1)S(1)}, u32[]{:S(2)}, u32[]{:S(2)}) collective-permute-start(bf16[256,256]{1,0:T(8,128)(2,1)S(1)} %get-tuple-element.211), channel_id=1, source_target_pairs={{0,2},{1,3},{2,0},{3,1},{4,6},{5,7},{6,4},{7,5},{8,10},{9,11},{10,... | collective-permute-start | bytes 393224 | tf_op jit(solution)/shard_map/ppermute | solution.py:48
  43.8 8.4 %collective-permute-start.13 = (bf16[256,256]{1,0:T(8,128)(2,1)S(1)}, bf16[256,256]{1,0:T(8,128)(2,1)S(1)}, u32[]{:S(2)}, u32[]{:S(2)}) collective-permute-start(bf16[256,256]{1,0:T(8,128)(2,1)S(1)} %get-tuple-element.212), channel_id=1, source_target_pairs={{0,6},{1,7},{2,4},{3,5},{4,2},{5,3},{6,0},{7,1},{8,14},{9,15},{10,... | collective-permute-start | bytes 393224 | tf_op jit(solution)/shard_map/ppermute | solution.py:48
  46.2 18.4 %collective-permute-start.4 = (bf16[128,1024]{1,0:T(8,128)(2,1)S(1)}, bf16[128,1024]{1,0:T(8,128)(2,1)S(1)}, u32[]{:S(2)}, u32[]{:S(2)}) collective-permute-start(bf16[128,1024]{1,0:T(8,128)(2,1)S(1)} %pad_maximum_fusion.2), channel_id=1, source_target_pairs={{0,6},{1,7},{2,4},{3,5},{4,2},{5,3},{6,0},{7,1},{8,14},{9,15},{10,... | collective-permute-start | bytes 786440 | tf_op jit(solution)/shard_map/ppermute | solution.py:48
  49.8 10.9 %collective-permute-start.12 = (bf16[512,256]{1,0:T(8,128)(2,1)S(1)}, bf16[512,256]{1,0:T(8,128)(2,1)S(1)}, u32[]{:S(2)}, u32[]{:S(2)}) collective-permute-start(bf16[512,256]{1,0:T(8,128)(2,1)S(1)} %pad_maximum_fusion.4), channel_id=1, source_target_pairs={{0,6},{1,7},{2,4},{3,5},{4,2},{5,3},{6,0},{7,1},{8,14},{9,15},{10,... | collective-permute-start | bytes 786440 | tf_op jit(solution)/shard_map/ppermute | solution.py:48
  52.2 8.4 %collective-permute-start.14 = (bf16[512,256]{1,0:T(8,128)(2,1)S(1)}, bf16[512,256]{1,0:T(8,128)(2,1)S(1)}, u32[]{:S(2)}, u32[]{:S(2)}) collective-permute-start(bf16[512,256]{1,0:T(8,128)(2,1)S(1)} %pad_maximum_fusion.5), channel_id=1, source_target_pairs={{0,2},{1,3},{2,0},{3,1},{4,6},{5,7},{6,4},{7,5},{8,10},{9,11},{10,... | collective-permute-start | bytes 786440 | tf_op jit(solution)/shard_map/ppermute | solution.py:48
  56.3 8.3 %collective-permute-start.6 = (bf16[128,1024]{1,0:T(8,128)(2,1)S(1)}, bf16[128,1024]{1,0:T(8,128)(2,1)S(1)}, u32[]{:S(2)}, u32[]{:S(2)}) collective-permute-start(bf16[128,1024]{1,0:T(8,128)(2,1)S(1)} %pad_maximum_fusion.3), channel_id=1, source_target_pairs={{0,2},{1,3},{2,0},{3,1},{4,6},{5,7},{6,4},{7,5},{8,10},{9,11},{10,... | collective-permute-start | bytes 786440 | tf_op jit(solution)/shard_map/ppermute | solution.py:48
  61.9 10.2 %collective-permute-start.15 = (bf16[1024,512]{1,0:T(8,128)(2,1)}, bf16[1024,512]{1,0:T(8,128)(2,1)S(1)}, u32[]{:S(2)}, u32[]{:S(2)}) collective-permute-start(bf16[1024,512]{1,0:T(8,128)(2,1)} %maximum_maximum_fusion.1), channel_id=1, source_target_pairs={{0,1},{1,0},{2,3},{3,2},{4,5},{5,4},{6,7},{7,6},{8,9},{9,8},{10,11... | collective-permute-start | bytes 3145736 | tf_op jit(solution)/shard_map/ppermute | solution.py:48
  65.8 7.1 %collective-permute-start.7 = (bf16[256,2048]{1,0:T(8,128)(2,1)}, bf16[256,2048]{1,0:T(8,128)(2,1)}, u32[]{:S(2)}, u32[]{:S(2)}) collective-permute-start(bf16[256,2048]{1,0:T(8,128)(2,1)} %maximum_maximum_fusion), channel_id=1, source_target_pairs={{0,1},{1,0},{2,3},{3,2},{4,5},{5,4},{6,7},{7,6},{8,9},{9,8},{10,11... | collective-permute-start | bytes 3145736 | tf_op jit(solution)/shard_map/ppermute | solution.py:48
  77.5 5.4 %collective-permute-start.31 = (bf16[2,64,512]{2,1,0:T(8,128)(2,1)S(1)}, bf16[2,64,512]{2,1,0:T(8,128)(2,1)S(1)}, u32[]{:S(2)}, u32[]{:S(2)}) collective-permute-start(bf16[2,64,512]{2,1,0:T(8,128)(2,1)S(1)} %get-tuple-element.144), channel_id=1, source_target_pairs={{0,64},{1,65},{2,66},{3,67},{4,68},{5,69},{6,70},{7,71},{8,72},{9,... | collective-permute-start | bytes 393224 | tf_op jit(solution)/shard_map/ppermute | solution.py:48
  81.5 4.7 %collective-permute-start.16 = (bf16[2,64,512]{2,1,0:T(8,128)(2,1)S(1)}, bf16[2,64,512]{2,1,0:T(8,128)(2,1)S(1)}, u32[]{:S(2)}, u32[]{:S(2)}) collective-permute-start(bf16[2,64,512]{2,1,0:T(8,128)(2,1)S(1)} %get-tuple-element.99), channel_id=1, source_target_pairs={{0,64},{1,65},{2,66},{3,67},{4,68},{5,69},{6,70},{7,71},{8,72},{9,... | collective-permute-start | bytes 393224 | tf_op jit(solution)/shard_map/ppermute | solution.py:48
  82.9 4.1 %collective-permute-start.32 = (bf16[2,64,512]{2,1,0:T(8,128)(2,1)S(1)}, bf16[2,64,512]{2,1,0:T(8,128)(2,1)S(1)}, u32[]{:S(2)}, u32[]{:S(2)}) collective-permute-start(bf16[2,64,512]{2,1,0:T(8,128)(2,1)S(1)} %get-tuple-element.145), channel_id=1, source_target_pairs={{64,128},{65,129},{66,130},{67,131},{68,132},{69,133},{70,134},{71... | collective-permute-start | bytes 393224 | tf_op jit(solution)/shard_map/ppermute | solution.py:48
  86.3 1.4 collective-permute-start.17
  87.0 1.4 collective-permute-start.33
  87.7 1.4 collective-permute-start.18
  88.4 1.4 collective-permute-start.34
  89.1 10.2 %collective-permute-start.19 = (bf16[2,64,512]{2,1,0:T(8,128)(2,1)S(1)}, bf16[2,64,512]{2,1,0:T(8,128)(2,1)S(1)}, u32[]{:S(2)}, u32[]{:S(2)}) collective-permute-start(bf16[2,64,512]{2,1,0:T(8,128)(2,1)S(1)} %get-tuple-element.102), channel_id=1, source_target_pairs={{192,288},{193,289},{194,290},{195,291},{196,292},{197,293},{198,2... | collective-permute-start | bytes 393224 | tf_op jit(solution)/shard_map/ppermute | solution.py:48
  90.0 12.8 %collective-permute-start.35 = (bf16[2,64,512]{2,1,0:T(8,128)(2,1)S(1)}, bf16[2,64,512]{2,1,0:T(8,128)(2,1)S(1)}, u32[]{:S(2)}, u32[]{:S(2)}) collective-permute-start(bf16[2,64,512]{2,1,0:T(8,128)(2,1)S(1)} %get-tuple-element.148), channel_id=1, source_target_pairs={{0,64},{1,65},{2,66},{3,67},{4,68},{5,69},{6,70},{7,71},{8,72},{9,... | collective-permute-start | bytes 393224 | tf_op jit(solution)/shard_map/ppermute | solution.py:48
  99.3 4.9 %collective-permute-start.20 = (bf16[2,64,512]{2,1,0:T(8,128)(2,1)S(1)}, bf16[2,64,512]{2,1,0:T(8,128)(2,1)S(1)}, u32[]{:S(2)}, u32[]{:S(2)}) collective-permute-start(bf16[2,64,512]{2,1,0:T(8,128)(2,1)S(1)} %get-tuple-element.103), channel_id=1, source_target_pairs={{0,64},{1,65},{2,66},{3,67},{4,68},{5,69},{6,70},{7,71},{8,72},{9,... | collective-permute-start | bytes 393224 | tf_op jit(solution)/shard_map/ppermute | solution.py:48
  100.6 4.2 %collective-permute-start.23 = (bf16[128,512]{1,0:T(8,128)(2,1)S(1)}, bf16[128,512]{1,0:T(8,128)(2,1)S(1)}, u32[]{:S(2)}, u32[]{:S(2)}) collective-permute-start(bf16[128,512]{1,0:T(8,128)(2,1)S(1)} %copy-done.3), channel_id=1, source_target_pairs={{448,480},{449,481},{450,482},{451,483},{452,484},{453,485},{454,4... | collective-permute-start | bytes 393224 | tf_op jit(solution)/shard_map/ppermute | solution.py:48
  102.8 2.4 collective-permute-start.36
  104.2 1.7 collective-permute-start.21
  105.2 1.4 collective-permute-start.37
  105.9 1.4 collective-permute-start.22
  106.6 1.4 collective-permute-start.38
  107.3 1.4 collective-permute-start.24
  108.0 1.4 collective-permute-start.39
  108.8 2.0 collective-permute-start.25
  109.5 43.2 %collective-permute-start.40 = (bf16[2,64,512]{2,1,0:T(8,128)(2,1)S(1)}, bf16[2,64,512]{2,1,0:T(8,128)(2,1)S(1)}, u32[]{:S(2)}, u32[]{:S(2)}) collective-permute-start(bf16[2,64,512]{2,1,0:T(8,128)(2,1)S(1)} %get-tuple-element.163), channel_id=1, source_target_pairs={{64,0},{65,1},{66,2},{67,3},{68,4},{69,5},{70,6},{71,7},{72,8},{73... | collective-permute-start | bytes 393224 | tf_op jit(solution)/shard_map/ppermute | solution.py:48
  110.8 43.2 %collective-permute-start.26 = (bf16[2,64,512]{2,1,0:T(8,128)(2,1)S(1)}, bf16[2,64,512]{2,1,0:T(8,128)(2,1)S(1)}, u32[]{:S(2)}, u32[]{:S(2)}) collective-permute-start(bf16[2,64,512]{2,1,0:T(8,128)(2,1)S(1)} %get-tuple-element.118), channel_id=1, source_target_pairs={{64,0},{65,1},{66,2},{67,3},{68,4},{69,5},{70,6},{71,7},{72,8},{73... | collective-permute-start | bytes 393224 | tf_op jit(solution)/shard_map/ppermute | solution.py:48
  152.6 2.1 collective-permute-start.41
  154.0 1.4 collective-permute-start.27
  154.7 1.4 collective-permute-start.42
  155.4 1.4 collective-permute-start.28
  156.1 1.4 collective-permute-start.43
  156.9 2.0 collective-permute-start.29
  157.6 52.5 %collective-permute-start.44 = (bf16[2,64,512]{2,1,0:T(8,128)(2,1)S(1)}, bf16[2,64,512]{2,1,0:T(8,128)(2,1)S(1)}, u32[]{:S(2)}, u32[]{:S(2)}) collective-permute-start(bf16[2,64,512]{2,1,0:T(8,128)(2,1)S(1)} %get-tuple-element.179), channel_id=1, source_target_pairs={{64,0},{65,1},{66,2},{67,3},{68,4},{69,5},{70,6},{71,7},{72,8},{73... | collective-permute-start | bytes 393224 | tf_op jit(solution)/shard_map/ppermute | solution.py:48
  158.9 55.2 %collective-permute-start.30 = (bf16[2,64,512]{2,1,0:T(8,128)(2,1)S(1)}, bf16[2,64,512]{2,1,0:T(8,128)(2,1)S(1)}, u32[]{:S(2)}, u32[]{:S(2)}) collective-permute-start(bf16[2,64,512]{2,1,0:T(8,128)(2,1)S(1)} %get-tuple-element.134), channel_id=1, source_target_pairs={{64,0},{65,1},{66,2},{67,3},{68,4},{69,5},{70,6},{71,7},{72,8},{73... | collective-permute-start | bytes 393224 | tf_op jit(solution)/shard_map/ppermute | solution.py:48
  216.4 4.6 %collective-permute-start.45 = (bf16[256,2048]{1,0:T(8,128)(2,1)S(1)}, bf16[256,2048]{1,0:T(8,128)(2,1)S(1)}, u32[]{:S(2)}, u32[]{:S(2)}) collective-permute-start(bf16[256,2048]{1,0:T(8,128)(2,1)S(1)} %get-tuple-element.192), channel_id=1, source_target_pairs={{0,1},{1,0},{2,3},{3,2},{4,5},{5,4},{6,7},{7,6},{8,9},{9,8},{10,11... | collective-permute-start | bytes 3145736 | tf_op jit(solution)/shard_map/ppermute | solution.py:48
  221.3 44.2 %copy-start.1 = (bf16[128,512]{1,0:T(8,128)(2,1)S(1)}, bf16[128,512]{1,0:T(8,128)(2,1)}, u32[]{:S(2)}) copy-start(bf16[128,512]{1,0:T(8,128)(2,1)} %param.5) | copy-start | bytes 393220
  241.5 22.5 %all-to-all-start.1 = ((bf16[8,8,2048]{2,1,0:T(8,128)(2,1)}), bf16[8,8,2048]{2,1,0:T(8,128)(2,1)S(1)}, u32[]{:S(2)}, u32[]{:S(2)}) async-start(bf16[8,8,2048]{2,1,0:T(8,128)(2,1)} %bitcast.15), calls=%async_computation.1 | async-start | bytes 524288 | tf_op jit(solution)/shard_map/all_to_all | solution.py:400
  (3 other events, 27.2 us)
